TPU v7x, 128 devices: a whole 4x4x4 slice. The times are simulated.
128 devices in a mesh: phase: 2 (over x_hi), seq: 64 (over z, y, x_lo, core).
Axes of the slice: x: 4 (x_hi: 2, x_lo: 2; x = x_hi * 2 + x_lo), y: 4, z: 4, core: 2. Of those that a mesh axis runs over, the one named last changes fastest.
Arguments:
- dec_in: bfloat16 [2, 512, 4096], P(None, None, 'seq'), may hold values from -6 to 6
- enc_kv: bfloat16 [2, 2, 8192, 8192], P('phase', None, 'seq'), may hold values from -15 to 15
- dec_seg: int32 [2, 512], replicated, may hold values from 0 to 3, never falling along the last dimension, each value on 1 to 256 neighbouring positions
- enc_seg: int32 [2, 8192], replicated, may hold values from 0 to 3, never falling along the last dimension, each value on 1 to 4096 neighbouring positions
- q_gain: float32 [2, 4096], P('phase', 'seq'), may hold values from 0.5 to 1.5
- o_gain: float32 [2, 4096], P('phase', 'seq'), may hold values from 1 to 8
- cotangent: bfloat16 [2, 512, 4096], P(None, None, 'seq'), may hold values from -6 to 6
Outputs:
- sect_out: bfloat16 [2, 2, 512, 4096], P('phase', None, None, 'seq')
- grad_kv: bfloat16 [2, 2, 8192, 8192], P('phase', None, 'seq')
- grad_q_gain: float32 [2, 4096], P('phase', 'seq')
- grad_o_gain: float32 [2, 4096], P('phase', 'seq')
Inputs may be any that keep to these rules, and one draw needn't show every extreme that they name: `dec_seg`: every one of the 4 documents has positions in both the decoder and the encoder of each micro-batch.
All inputs are finite; a program needn't handle non-finite values.
Results may differ from a plain program's by a relative error of at most 0.0075.
The roundings to bfloat16 on the way count: a program that leaves them out, or rounds other values in their place, can miss the bound.
Values may be sent and summed in bfloat16 or wider, within the bound.
No kernel may reach another device: no remote copies, remote signals or barrier semaphores. Data moves between devices by JAX's collectives and lax.ppermute only.
A program may use at most 192 MiB of HBM per device.

v0:
```python
import functools
import math

import jax
import jax.numpy as jnp
from jax import lax
from jax.experimental import pallas as pl
from jax.experimental.pallas import tpu as pltpu
from jax.sharding import PartitionSpec as P

D = 4096
HEAD = 64
EPS = 1e-06
NEG = -1e30
DOCS = 4
TILE = 256
CHUNK = 512
UNROLL = 4
TAIL = 16
SCALE = 1.0 / math.sqrt(HEAD)
LOG2 = SCALE * math.log2(math.e)
BOTH = ("phase", "seq")
F32 = jnp.float32
BF16 = jnp.bfloat16


def dot(a, b, ca, cb):
    return lax.dot_general(a, b, (((ca,), (cb,)), ((), ())), preferred_element_type=F32)


def vmem(shape, index):
    return pl.BlockSpec(shape, lambda i: index)


def whole(shape):
    return vmem(shape, (0,) * len(shape))


SMEM = pl.BlockSpec(memory_space=pltpu.SMEM)
PARAMS = dict(
    compiler_params=pltpu.CompilerParams(
        dimension_semantics=("arbitrary",), vmem_limit_bytes=48 * 1024 * 1024
    )
)


def pack_kernel(phase_ref, kv_ref, x_ref, out_ref):
    heads = kv_ref.shape[2] // (2 * HEAD)
    for h in range(heads):
        out_ref[h, 0:128, :] = kv_ref[0, :, h * 128 : (h + 1) * 128]
    x = x_ref[0, pl.ds(phase_ref[0] * 256, 256), :].astype(F32)
    x = jnp.concatenate([x, jnp.zeros_like(x)], axis=1)
    xt = jnp.transpose(x)
    total = jnp.sum(xt * xt, axis=0, keepdims=True)
    rows = []
    for _ in range(3):
        part = total.astype(BF16)
        partf = part.astype(F32)
        rows += [partf[:, 0:128], partf[:, 128:256]]
        total = total - partf
    rows.append(jnp.zeros((TAIL - 6, 128), F32))
    tail = jnp.concatenate(rows, axis=0).astype(BF16)
    for h in range(heads):
        out_ref[h, 128 : 128 + TAIL, :] = tail


def pack(phase, kv, dec_in):
    micro, rows, feats = kv.shape
    parts = 4
    heads = feats // 128 // parts
    return pl.pallas_call(
        pack_kernel,
        grid=(micro * parts,),
        in_specs=[
            SMEM,
            pl.BlockSpec((1, rows, feats // parts), lambda i: (i // parts, 0, i % parts)),
            pl.BlockSpec((1, dec_in.shape[1], HEAD), lambda i: (i // parts, 0, 0)),
        ],
        out_specs=pl.BlockSpec((heads, rows + TAIL, 128), lambda i: (i, 0, 0)),
        out_shape=jax.ShapeDtypeStruct((micro * parts * heads, rows + TAIL, 128), BF16),
        name="pack",
        **PARAMS,
    )(phase, kv, dec_in)


def unpack_kernel(in_ref, out_ref):
    for h in range(in_ref.shape[0]):
        out_ref[0, :, h * 128 : (h + 1) * 128] = in_ref[h]


def unpack(blocks, micro):
    count, rows, _ = blocks.shape
    parts = 4
    heads = count // micro // parts
    return pl.pallas_call(
        unpack_kernel,
        grid=(micro * parts,),
        in_specs=[pl.BlockSpec((heads, rows, 128), lambda i: (i, 0, 0))],
        out_specs=pl.BlockSpec((1, rows, heads * 128), lambda i: (i // parts, 0, i % parts)),
        out_shape=jax.ShapeDtypeStruct((micro, rows, parts * heads * 128), BF16),
        name="unpack",
        **PARAMS,
    )(blocks)


def items_of(positions):
    most = positions // CHUNK + DOCS - 1
    return (most + UNROLL - 1) // UNROLL * UNROLL


def work(positions, body):
    def some(i, carry):
        for u in range(UNROLL):
            body(i * UNROLL + u)
        return carry

    lax.fori_loop(0, items_of(positions) // UNROLL, some, 0)


def chunk_of(kv_ref, c):
    per = CHUNK // 128
    return kv_ref[0, pl.ds(c * per, per)].reshape(CHUNK, 128)


def lanes(d):
    return slice(d * TILE, (d + 1) * TILE)


def logits(product, c, first, last):
    position = lax.broadcasted_iota(jnp.int32, (CHUNK, TILE), 0) + c * CHUNK
    allowed = (position >= first) & (position < last)
    return jnp.where(allowed, product * LOG2, NEG)


def forward_items(plan_ref, kv_ref, query, lse, total, query_ref, top_ref, norm_ref, store):
    for d in range(DOCS):
        query_ref[d] = query[:, lanes(d)]
    query_ref[DOCS] = jnp.zeros((128, TILE), BF16)
    top_ref[...] = jnp.full(top_ref.shape, NEG, F32)
    norm_ref[...] = jnp.zeros(norm_ref.shape, F32)
    total[...] = jnp.zeros(total.shape, F32)
    positions = kv_ref.shape[1] * 128

    def stats(k):
        c, d = plan_ref[0, k], plan_ref[1, k]
        product = dot(chunk_of(kv_ref, c), query_ref[d], 1, 0)
        scores = logits(product, c, plan_ref[2, k], plan_ref[3, k])
        store[k] = scores
        groups = scores.reshape(CHUNK // 8, 8, TILE)
        top = jnp.max(groups, axis=0)
        norm = jnp.sum(jnp.exp2(groups - top[None]), axis=0)
        before = top_ref[d]
        now = jnp.maximum(before, top)
        norm_ref[d] = norm_ref[d] * jnp.exp2(before - now) + norm * jnp.exp2(top - now)
        top_ref[d] = now

    work(positions, stats)
    for d in range(DOCS + 1):
        top = top_ref[d]
        peak = jnp.max(top, axis=0, keepdims=True)
        norm = jnp.sum(norm_ref[d] * jnp.exp2(top - peak), axis=0, keepdims=True)
        lse[d] = jnp.broadcast_to(peak + jnp.log2(norm), (8, TILE))

    def gather(k):
        c, d = plan_ref[0, k], plan_ref[1, k]
        probs = jnp.exp2(store[k] - lse[d, 0:1])
        weights = probs.astype(BF16)
        left = (probs - weights.astype(F32)).astype(BF16)
        total[d] += dot(chunk_of(kv_ref, c), jnp.concatenate([weights, left], axis=1), 0, 0)

    work(positions, gather)


def forward_scratch(items):
    return [
        pltpu.VMEM((DOCS + 1, 128, 2 * TILE), F32),
        pltpu.VMEM((DOCS + 1, 128, TILE), BF16),
        pltpu.VMEM((DOCS + 1, 8, TILE), F32),
        pltpu.VMEM((DOCS + 1, 8, TILE), F32),
        pltpu.VMEM((items, CHUNK, TILE), F32),
    ]


def attended(total, d):
    attn = total[d, HEAD:, :TILE]
    return attn, attn + total[d, HEAD:, TILE:]


def pad_low(a):
    return jnp.concatenate([a, jnp.zeros_like(a)], axis=0)


def pad_high(a):
    return jnp.concatenate([jnp.zeros_like(a), a], axis=0)


def upright(a):
    return jnp.transpose(a.astype(F32)).astype(BF16)


def normed_query(xt, total, qgain):
    inv = lax.rsqrt(total / D + EPS)
    return inv, (xt * inv * qgain).astype(BF16)


def thirds(value):
    parts = []
    for _ in range(3):
        part = value.astype(BF16).astype(F32)
        parts.append(part)
        value = value - part
    return parts


def forward_kernel(
    plan_ref, kv_ref, tails_ref, xt_ref, place_ref, live_ref, qgain_ref, ogain_ref,
    out_ref, sums_ref, lse_ref, attn_ref, exact_ref, inv_ref,
    total_ref, query_ref, top_ref, norm_ref, store,
):
    tails = jnp.sum(tails_ref[...].astype(F32), axis=1)
    pieces = []
    for half in range(2):
        pieces += [
            tails[half, j : j + 1] + tails[half, j + 2 : j + 3] + tails[half, j + 4 : j + 5]
            for j in range(2)
        ]
    parts = thirds(jnp.concatenate(pieces, axis=1))
    parts.append(jnp.zeros((13, parts[0].shape[1]), F32))
    moved = dot(jnp.concatenate(parts, axis=0).astype(BF16), place_ref[...], 1, 0)
    total = jnp.sum(moved, axis=0, keepdims=True)
    xt = xt_ref[...].astype(F32)
    inv, query = normed_query(xt, total, qgain_ref[...])
    inv_ref[...] = inv
    forward_items(
        plan_ref, kv_ref, pad_low(query), lse_ref, total_ref, query_ref, top_ref, norm_ref, store
    )
    for d in range(DOCS):
        s = lanes(d)
        attn, exact = attended(total_ref, d)
        attn_ref[:, s] = attn
        exact_ref[:, s] = exact
        out = (xt[:, s] + ogain_ref[...] * attn) * live_ref[:, s]
        out_ref[:, s] = out.astype(BF16)
    out = out_ref[...].astype(F32)
    sums_ref[...] = jnp.broadcast_to(jnp.sum(out * out, axis=0, keepdims=True), sums_ref.shape)


def call(kernel, name, ins, outs, scratch, args, **more):
    return pl.pallas_call(
        kernel,
        grid=(1,),
        in_specs=ins,
        out_specs=[spec for spec, _ in outs],
        out_shape=[shape for _, shape in outs],
        scratch_shapes=scratch,
        name=name,
        **more,
        **PARAMS,
    )(*args)


def plain(shape, dtype=F32):
    return whole(shape), jax.ShapeDtypeStruct(shape, dtype)


def forward(plan, received, xt, place, live, qgain, ogain):
    width = xt.shape[1]
    blocks = received.shape[1]
    ins = [
        SMEM,
        vmem((1, blocks, 128, 128), (0, 0, 0, 0)),
        vmem((2, blocks, TAIL, 128), (0, 0, 128 // TAIL, 0)),
        whole((HEAD, width)),
        whole(place.shape),
        whole((1, width)),
        whole((HEAD, 1)),
        whole((HEAD, 1)),
    ]
    outs = [
        plain((HEAD, width), BF16),
        plain((blocks, width)),
        plain((DOCS + 1, 8, TILE)),
        plain((HEAD, width)),
        plain((HEAD, width)),
        plain((1, width)),
    ]
    return call(
        forward_kernel, "forward", ins, outs, forward_scratch(items_of(blocks * 128)),
        (plan, received, received, xt, place, live, qgain, ogain),
    )


def backward_step(keyval, probs, grad_probs, delta, pair, grad_kv_ref, c):
    grad_scores = (probs * (grad_probs - delta)).astype(BF16)
    left = jnp.concatenate([grad_scores, probs.astype(BF16)], axis=1)
    per = CHUNK // 128
    held = grad_kv_ref[0, pl.ds(c * per, per)].reshape(CHUNK, 128)
    added = held.astype(F32) + dot(left, pair, 1, 0)
    grad_kv_ref[0, pl.ds(c * per, per)] = added.astype(BF16).reshape(per, 128, 128)
    return dot(keyval, grad_scores, 0, 0)[:HEAD]


def fill_pairs(pair_ref, delta_ref, query, grad_out, deltas):
    keys_side = upright(query.astype(F32) * SCALE)
    values_side = upright(grad_out)
    for d in range(DOCS):
        s = lanes(d)
        pair_ref[d] = jnp.concatenate([keys_side[s], values_side[s]], axis=0)
        delta_ref[d] = jnp.broadcast_to(deltas[:, s], (8, TILE))
    pair_ref[DOCS] = jnp.zeros((2 * TILE, 128), BF16)
    delta_ref[DOCS] = jnp.zeros((8, TILE), F32)


def backward_scratch():
    return [
        pltpu.VMEM((DOCS + 1, 2 * TILE, 128), BF16),
        pltpu.VMEM((DOCS + 1, 8, TILE), F32),
        pltpu.VMEM((DOCS + 1, HEAD, TILE), F32),
    ]


def lined_up(ref):
    return jnp.concatenate([ref[d] for d in range(DOCS)], axis=1)


def middle_kernel(
    plan_ref, kv_ref, sums_ref, xt_ref, live_ref, qgain_ref, ogain_ref, gt_ref,
    grad_kv_ref, out_ref, cross_ref, grad_norm_ref, inv_ref, grad_qg_ref, grad_og_ref,
    total_ref, query_ref, top_ref, norm_ref, store,
    pair_ref, delta_ref, grad_query_ref, lse_ref, grad_ref,
):
    grad_kv_ref[...] = jnp.zeros_like(grad_kv_ref)
    grad_query_ref[...] = jnp.zeros_like(grad_query_ref)
    total = jnp.sum(sums_ref[...], axis=0, keepdims=True)
    xt = xt_ref[...].astype(F32)
    inv, low = normed_query(xt, total, qgain_ref[...])
    inv_ref[...] = inv
    query = pad_low(low)
    grad = gt_ref[...].astype(F32)
    grad_low = (grad * ogain_ref[...]).astype(BF16)
    grad_out = pad_high(grad_low)
    for d in range(DOCS):
        grad_ref[d] = grad_out[:, lanes(d)]
    grad_ref[DOCS] = jnp.zeros((128, TILE), BF16)
    forward_items(
        plan_ref, kv_ref, query, lse_ref, total_ref, query_ref, top_ref, norm_ref, store
    )
    both = [attended(total_ref, d) for d in range(DOCS)]
    attn = jnp.concatenate([a for a, _ in both], axis=1)
    exact = jnp.concatenate([e for _, e in both], axis=1)
    deltas = jnp.sum(grad_low.astype(F32) * exact, axis=0, keepdims=True)
    fill_pairs(pair_ref, delta_ref, query, grad_out, deltas)

    def back(k):
        c, d = plan_ref[0, k], plan_ref[1, k]
        keyval = chunk_of(kv_ref, c)
        probs = jnp.exp2(store[k] - lse_ref[d, 0:1])
        grad_probs = dot(keyval, grad_ref[d], 1, 0)
        grad_query_ref[d] += backward_step(
            keyval, probs, grad_probs, delta_ref[d, 0:1], pair_ref[d], grad_kv_ref, c
        )

    work(kv_ref.shape[1] * 128, back)
    out_ref[...] = ((xt + ogain_ref[...] * attn) * live_ref[...]).astype(BF16)
    grad_query = lined_up(grad_query_ref) * SCALE
    grad_norm = grad_query * qgain_ref[...]
    grad_norm_ref[...] = grad_norm
    cross = jnp.sum(grad_norm * xt, axis=0, keepdims=True)
    cross_ref[...] = jnp.broadcast_to(cross, cross_ref.shape)
    grad_qg_ref[...] = jnp.sum(grad_query * (xt * inv), axis=1, keepdims=True)
    grad_og_ref[...] = jnp.sum(grad * attn, axis=1, keepdims=True)


def middle(plan, received, sums, xt, live, qgain, ogain, gt):
    width = xt.shape[1]
    blocks = received.shape[1]
    ins = [
        SMEM,
        vmem((1, blocks, 128, 128), (1, 0, 0, 0)),
        whole((blocks, width)),
        whole((HEAD, width)),
        whole((1, width)),
        whole((HEAD, 1)),
        whole((HEAD, 1)),
        whole((HEAD, width)),
    ]
    outs = [
        (
            vmem((1, blocks, 128, 128), (1, 0, 0, 0)),
            jax.ShapeDtypeStruct((2, blocks, 128, 128), BF16),
        ),
        plain((HEAD, width), BF16),
        plain((blocks, width)),
        plain((HEAD, width)),
        plain((1, width)),
        plain((HEAD, 1)),
        plain((HEAD, 1)),
    ]
    scratch = forward_scratch(items_of(blocks * 128)) + backward_scratch()
    scratch += [
        pltpu.VMEM((DOCS + 1, 8, TILE), F32),
        pltpu.VMEM((DOCS + 1, 128, TILE), BF16),
    ]
    return call(
        middle_kernel, "middle", ins, outs, scratch,
        (plan, received, sums, xt, live, qgain, ogain, gt),
    )


def backward_kernel(
    plan_ref, kv_ref, cross_ref, gt_ref, grad_norm_ref, xt1_ref, inv1_ref,
    xt_ref, inv_ref, lse_ref, attn_ref, exact_ref, qgain_ref, ogain_ref, held_ref,
    grad_kv_ref, grad_qg_ref, grad_og_ref, pair_ref, delta_ref, grad_query_ref, both_ref,
):
    del held_ref
    grad_kv_ref[...] = jnp.zeros_like(grad_kv_ref)
    grad_query_ref[...] = jnp.zeros_like(grad_query_ref)
    cross = jnp.sum(cross_ref[...], axis=0, keepdims=True)
    inv1 = inv1_ref[...]
    xt1 = xt1_ref[...].astype(F32)
    grad = gt_ref[...].astype(F32) + inv1 * grad_norm_ref[...]
    grad = (grad - xt1 * (inv1 * inv1 * inv1) * (cross / D)).astype(BF16).astype(F32)
    grad_low = (grad * ogain_ref[...]).astype(BF16)
    grad_out = pad_high(grad_low)
    grad_og_ref[...] = jnp.sum(grad * attn_ref[...], axis=1, keepdims=True)
    deltas = jnp.sum(grad_low.astype(F32) * exact_ref[...], axis=0, keepdims=True)
    normed = xt_ref[...].astype(F32) * inv_ref[...]
    query = pad_low((normed * qgain_ref[...]).astype(BF16))
    fill_pairs(pair_ref, delta_ref, query, grad_out, deltas)
    for d in range(DOCS):
        both_ref[d] = jnp.concatenate([query[:, lanes(d)], grad_out[:, lanes(d)]], axis=1)
    both_ref[DOCS] = jnp.zeros((128, 2 * TILE), BF16)

    def back(k):
        c, d = plan_ref[0, k], plan_ref[1, k]
        keyval = chunk_of(kv_ref, c)
        product = dot(keyval, both_ref[d], 1, 0)
        scores = logits(product[:, :TILE], c, plan_ref[2, k], plan_ref[3, k])
        probs = jnp.exp2(scores - lse_ref[d, 0:1])
        grad_query_ref[d] += backward_step(
            keyval, probs, product[:, TILE:], delta_ref[d, 0:1], pair_ref[d], grad_kv_ref, c
        )

    work(kv_ref.shape[1] * 128, back)
    grad_query = lined_up(grad_query_ref) * SCALE
    grad_qg_ref[...] = jnp.sum(grad_query * normed, axis=1, keepdims=True)


def backward(
    plan, received, cross, gt, grad_norm, xt1, inv1, xt, inv, lse, attn, exact, qgain, ogain, held
):
    width = xt.shape[1]
    blocks = received.shape[1]
    ins = [
        SMEM,
        vmem((1, blocks, 128, 128), (0, 0, 0, 0)),
        whole((blocks, width)),
        whole((HEAD, width)),
        whole((HEAD, width)),
        whole((HEAD, width)),
        whole((1, width)),
        whole((HEAD, width)),
        whole((1, width)),
        whole(lse.shape),
        whole((HEAD, width)),
        whole((HEAD, width)),
        whole((HEAD, 1)),
        whole((HEAD, 1)),
        pl.BlockSpec(memory_space=pl.ANY),
    ]
    outs = [
        (
            vmem((1, blocks, 128, 128), (0, 0, 0, 0)),
            jax.ShapeDtypeStruct(held.shape, BF16),
        ),
        plain((HEAD, 1)),
        plain((HEAD, 1)),
    ]
    scratch = backward_scratch() + [pltpu.VMEM((DOCS + 1, 128, 2 * TILE), BF16)]
    return call(
        backward_kernel, "backward", ins, outs, scratch,
        (plan, received, cross, gt, grad_norm, xt1, inv1, xt, inv, lse, attn, exact,
         qgain, ogain, held),
        input_output_aliases={14: 0},
    )


def runs(seg):
    counts = [jnp.sum((seg < d).astype(jnp.int32)) for d in range(1, DOCS)]
    return jnp.stack([jnp.int32(0)] + counts + [jnp.int32(seg.shape[0])])


def plan_of(kseg):
    edges = runs(kseg)
    first, last = edges[:-1], edges[1:]
    start = first // CHUNK
    count = (last + (CHUNK - 1)) // CHUNK - start
    ends = jnp.cumsum(count)
    k = jnp.arange(items_of(kseg.shape[0]), dtype=jnp.int32)
    doc = jnp.sum((k[:, None] >= ends[None, :]).astype(jnp.int32), axis=1)
    chunk, low, high = jnp.zeros_like(k), jnp.zeros_like(k), jnp.full_like(k, kseg.shape[0])
    for d in range(DOCS):
        here = doc == d
        chunk = jnp.where(here, start[d] + k - (ends[d] - count[d]), chunk)
        low = jnp.where(here, first[d], low)
        high = jnp.where(here, last[d], high)
    return jnp.stack([chunk, doc, low, high])


def place_of(qseg):
    edges = runs(qseg)
    lane = jnp.arange(TILE, dtype=jnp.int32)
    row = (edges[:-1, None] + lane[None, :]).reshape(1, DOCS * TILE)
    live = (lane[None, :] < (edges[1:] - edges[:-1])[:, None]).reshape(1, DOCS * TILE)
    rows = jnp.arange(qseg.shape[0], dtype=jnp.int32)[:, None]
    return ((rows == row) & live).astype(BF16), live.astype(F32)


def placed(x, place):
    return lax.dot_general(
        x, place, (((0,), (0,)), ((), ())), preferred_element_type=F32
    ).astype(BF16)


def taken(xt, place):
    return lax.dot_general(
        place, xt, (((1,), (1,)), ((), ())), preferred_element_type=F32
    ).astype(BF16)


def swap(value):
    return lax.ppermute(value, "phase", [(0, 1), (1, 0)])


def spread(value):
    return lax.all_to_all(value, "seq", 0, 0, tiled=True)


def local(dec_in, enc_kv, dec_seg, enc_seg, q_gain, o_gain, cotangent):
    phase = lax.axis_index("phase")
    first_phase = phase == 0
    micro = dec_in.shape[0]
    positions = enc_seg.shape[1]
    blocks = positions // 128

    sent = pack(phase.reshape(1), enc_kv[0], dec_in)
    own = jnp.concatenate([q_gain, o_gain], axis=0)
    other = swap(own)
    received = lax.all_to_all(sent, BOTH, 0, 0, tiled=True)
    received = received.reshape(2, blocks, 128 + TAIL, 128)

    gains0 = jnp.where(first_phase, own, other)
    gains1 = jnp.where(first_phase, other, own)
    qgain0, ogain0 = gains0[0][:, None], gains0[1][:, None]
    qgain1, ogain1 = gains1[0][:, None], gains1[1][:, None]
    qseg = lax.dynamic_index_in_dim(dec_seg, phase, 0, keepdims=False)
    kseg = lax.dynamic_index_in_dim(enc_seg, phase, 0, keepdims=False)
    plan = plan_of(kseg)
    place, live = place_of(qseg)
    xt0 = placed(lax.dynamic_index_in_dim(dec_in, phase, 0, keepdims=False), place)
    gt = placed(lax.dynamic_index_in_dim(cotangent, phase, 0, keepdims=False), place)

    xt1, sums, lse0, attn0, exact0, inv0 = forward(
        plan, received, xt0, place, live, qgain0, ogain0
    )
    sums = spread(sums)
    grad_kv, xt2, cross, grad_norm, inv1, grad_qg1, grad_og1 = middle(
        plan, received, sums, xt1, live, qgain1, ogain1, gt
    )
    cross = spread(cross)
    grad_kv, grad_qg0, grad_og0 = backward(
        plan, received, cross, gt, grad_norm, xt1, inv1, xt0, inv0, lse0, attn0, exact0,
        qgain0, ogain0, grad_kv,
    )
    rows_back = lax.all_to_all(
        grad_kv.reshape(2 * blocks, 128, 128), BOTH, 0, 0, tiled=True
    )
    grad_rows = unpack(rows_back, micro)

    out0, out1 = taken(xt1, place), taken(xt2, place)
    mine = jnp.where(first_phase, out0, out1)
    theirs = swap(jnp.where(first_phase, out1, out0))
    sect_out = jnp.where(
        first_phase, jnp.stack([mine, theirs]), jnp.stack([theirs, mine])
    )
    grads0 = jnp.concatenate([grad_qg0, grad_og0], axis=1).T
    grads1 = jnp.concatenate([grad_qg1, grad_og1], axis=1).T
    grads = jnp.where(first_phase, grads0, grads1) + swap(
        jnp.where(first_phase, grads1, grads0)
    )
    return (sect_out[None], grad_rows[None], grads[0:1], grads[1:2])


def solution(mesh):
    in_specs = (
        P(None, None, "seq"),
        P("phase", None, "seq", None),
        P(),
        P(),
        P("phase", "seq"),
        P("phase", "seq"),
        P(None, None, "seq"),
    )
    out_specs = (
        P("phase", None, None, "seq"),
        P("phase", None, "seq", None),
        P("phase", "seq"),
        P("phase", "seq"),
    )
    return jax.shard_map(local, mesh=mesh, in_specs=in_specs, out_specs=out_specs, check_vma=False)
```

profile of v0, /device:TPU:0, one launch (start us, length us, event | category | flops | bytes accessed | tf_op | source)
XLA Modules:
  0.0 215.5 jit_solution(11180853731139105963)
XLA Ops:
  0.7 1.1 copy.34.x_ref
  1.8 2.2 %copy-done.2 = bf16[1,2,128,8192]{3,2,1,0:T(8,128)(2,1)S(1)} copy-done((bf16[1,2,128,8192]{3,2,1,0:T(8,128)(2,1)S(1)}, bf16[1,2,128,8192]{3,2,1,0:T(8,128)(2,1)}, u32[]{:S(2)}) %copy-start.2) | copy-done | bytes 4194328
  4.0 4.3 %pack.1 = bf16[128,144,128]{2,1,0:T(8,128)(2,1)} custom-call(s32[1]{0:T(128)} %bitcast.23.phase_ref, bf16[2,128,8192]{2,1,0:T(8,128)(2,1)S(1)} %bitcast.70, bf16[2,512,64]{2,1,0:T(8,128)(2,1)S(1)} %copy.34.x_ref), custom_call_target="tpu_custom_call" | custom-call | tf_op jit(solution)/shard_map/pack/pallas_call | solution.py:71
  8.3 11.6 %all-to-all-start = ((bf16[128,144,128]{2,1,0:T(8,128)(2,1)}), bf16[128,144,128]{2,1,0:T(8,128)(2,1)}, u32[]{:S(2)}, u32[]{:S(2)}) async-start(bf16[128,144,128]{2,1,0:T(8,128)(2,1)} %pack.1), calls=%async_computation | async-start | bytes 9437184 | tf_op jit(solution)/shard_map/all_to_all | solution.py:549
  20.0 2.5 %collective-permute-start = (f32[2,64]{1,0:T(2,128)S(1)}, f32[2,64]{1,0:T(2,128)S(1)}, u32[]{:S(2)}, u32[]{:S(2)}) collective-permute-start(f32[2,64]{1,0:T(2,128)S(1)} %pad_maximum_fusion), channel_id=1, source_target_pairs={{0,64},{64,0},{1,65},{65,1},{2,66},{66,2},{3,67},{67,3},{4,68},{68... | collective-permute-start | bytes 1544 | tf_op jit(solution)/shard_map/ppermute | solution.py:532
  23.2 2.0 fusion.52
  26.1 1.9 add_subtract_fusion
  28.2 2.0 fusion.51
  36.6 4.5 %fusion.48 = (s32[1,20]{1,0:T(1,128)S(1)}, s32[1,20]{1,0:T(1,128)S(1)}, s32[1,20]{1,0:T(1,128)S(1)}) fusion(s32[]{:T(128)S(6)} %sub.106, s32[]{:T(128)} %bitcast.20, s32[]{:T(128)S(6)} %sub.103, s32[]{:T(128)} %bitcast.17, s32[]{:T(128)S(6)} %sub.100, s32[]{:T(128)} %bitcast.14, s32[]{:T(128)S(6)} %sub.97, s32[]{:T(128)} %bitcast.11, ...), kind=kLoop, calls=%fused_computation.82 | loop fusion | flops 460 | bytes 364 | tf_op jit(solution)/shard_map/jit(_where)/select_n | solution.py:504
  42.1 31.4 %collective-permute-done = f32[2,64]{1,0:T(2,128)S(1)} collective-permute-done((f32[2,64]{1,0:T(2,128)S(1)}, f32[2,64]{1,0:T(2,128)S(1)}, u32[]{:S(2)}, u32[]{:S(2)}) %collective-permute-start) | collective-permute-done | bytes 544 | tf_op jit(solution)/shard_map/ppermute | solution.py:532
  73.8 4.4 %all-to-all-done = bf16[128,144,128]{2,1,0:T(8,128)(2,1)} async-done(((bf16[128,144,128]{2,1,0:T(8,128)(2,1)}), bf16[128,144,128]{2,1,0:T(8,128)(2,1)}, u32[]{:S(2)}, u32[]{:S(2)}) %all-to-all-start) | async-done | bytes 4718624 | tf_op jit(solution)/shard_map/all_to_all | solution.py:549
  78.2 9.4 %forward.1 = (bf16[64,1024]{1,0:T(8,128)(2,1)S(1)}, f32[64,1024]{1,0:T(8,128)S(1)}, f32[5,8,256]{2,1,0:T(8,128)S(1)}, f32[64,1024]{1,0:T(8,128)S(1)}, f32[64,1024]{1,0:T(8,128)S(1)}, /*index=5*/f32[1,1024]{1,0:T(1,128)S(1)}) custom-call(s32[4,20]{1,0:T(4,128)S(1)} %pad_add_fusion.plan_ref, bf16[2,64,144,128]{3,2,1,0:T(8,128)(2,1)} %bitcast.25.kv_ref.tails_ref, ...), custom_call_target="tpu_custom_call" | custom-call | tf_op jit(solution)/shard_map/forward/pallas_call | solution.py:249
  88.6 6.8 %all-to-all-start.1 = ((f32[64,1,1024]{2,1,0:T(1,128)}), f32[64,1,1024]{2,1,0:T(1,128)S(1)}, u32[]{:S(2)}, u32[]{:S(2)}) async-start(f32[64,1,1024]{2,1,0:T(1,128)} %copy.37), calls=%async_computation.1 | async-start | bytes 524288 | tf_op jit(solution)/shard_map/all_to_all | solution.py:536
  96.1 9.2 %all-to-all-done.1 = f32[64,1,1024]{2,1,0:T(1,128)S(1)} async-done(((f32[64,1,1024]{2,1,0:T(1,128)}), f32[64,1,1024]{2,1,0:T(1,128)S(1)}, u32[]{:S(2)}, u32[]{:S(2)}) %all-to-all-start.1) | async-done | bytes 262176 | tf_op jit(solution)/shard_map/all_to_all | solution.py:536
  105.4 16.9 %middle.1 = (bf16[2,64,128,128]{3,2,1,0:T(8,128)(2,1)S(1)}, bf16[64,1024]{1,0:T(8,128)(2,1)S(1)}, f32[64,1024]{1,0:T(8,128)S(1)}, f32[64,1024]{1,0:T(8,128)S(1)}...) custom-call(s32[4,20]{1,0:T(4,128)S(1)} %pad_add_fusion.plan_ref, ...), custom_call_target="tpu_custom_call" | custom-call | tf_op jit(solution)/shard_map/middle/pallas_call | solution.py:249
  122.6 14.1 %all_to_all.32 = f32[64,1,1024]{2,1,0:T(1,128)S(1)} all-to-all(f32[64,1,1024]{2,1,0:T(1,128)S(1)} %copy.40), channel_id=1, replica_groups=mesh['phase'=2,'seq'=64] {'seq'}, dimensions={0} | all-to-all | bytes 524288 | tf_op jit(solution)/shard_map/all_to_all | solution.py:536
  136.8 10.0 %backward.1 = (bf16[2,64,128,128]{3,2,1,0:T(8,128)(2,1)S(1)}, f32[64,1]{1,0:T(8,128)S(1)}, f32[64,1]{1,0:T(8,128)S(1)}) custom-call(s32[4,20]{1,0:T(4,128)S(1)} %pad_add_fusion.plan_ref, bf16[2,64,144,128]{3,2,1,0:T(8,128)(2,1)} %bitcast.25.kv_ref.tails_ref, f32[64,1024]{1,0:T(8,128)S(1)} %bitcast.71, ...), custom_call_target="tpu_custom_call", output_to_operand_aliasing={{0}: (14, {})} | custom-call | tf_op jit(solution)/shard_map/backward/pallas_call | solution.py:249
  146.7 2.0 copy-done.1
  148.8 6.9 %all-to-all-start.3 = ((bf16[128,128,128]{2,1,0:T(8,128)(2,1)}), bf16[128,128,128]{2,1,0:T(8,128)(2,1)}, u32[]{:S(2)}, u32[]{:S(2)}) async-start(bf16[128,128,128]{2,1,0:T(8,128)(2,1)} %bitcast.69), calls=%async_computation.3 | async-start | bytes 8388608 | tf_op jit(solution)/shard_map/all_to_all | solution.py:575
  157.0 2.5 %collective-permute-start.1 = (bf16[512,64]{0,1:T(8,128)(2,1)S(1)}, bf16[512,64]{0,1:T(8,128)(2,1)S(1)}, u32[]{:S(2)}, u32[]{:S(2)}) collective-permute-start(bf16[512,64]{0,1:T(8,128)(2,1)S(1)} %get-tuple-element.51), channel_id=1, source_target_pairs={{0,64},{64,0},{1,65},{65,1},{2,66},{66,2},{3,67},{67,3},{4,68},{68... | collective-permute-start | bytes 196616 | tf_op jit(solution)/shard_map/ppermute | solution.py:532
  159.6 1.2 collective-permute-start.2
  160.8 43.5 %collective-permute-done.1 = bf16[512,64]{0,1:T(8,128)(2,1)S(1)} collective-permute-done((bf16[512,64]{0,1:T(8,128)(2,1)S(1)}, bf16[512,64]{0,1:T(8,128)(2,1)S(1)}, u32[]{:S(2)}, u32[]{:S(2)}) %collective-permute-start.1) | collective-permute-done | bytes 65568 | tf_op jit(solution)/shard_map/ppermute | solution.py:532
  205.5 3.1 %all-to-all-done.3.in_ref = bf16[128,128,128]{2,1,0:T(8,128)(2,1)} async-done(((bf16[128,128,128]{2,1,0:T(8,128)(2,1)}), bf16[128,128,128]{2,1,0:T(8,128)(2,1)}, u32[]{:S(2)}, u32[]{:S(2)}) %all-to-all-start.3) | async-done | bytes 4194336 | tf_op jit(solution)/shard_map/all_to_all | solution.py:575
  208.6 7.0 %unpack.1 = bf16[2,128,8192]{2,1,0:T(8,128)(2,1)} custom-call(bf16[128,128,128]{2,1,0:T(8,128)(2,1)} %all-to-all-done.3.in_ref), custom_call_target="tpu_custom_call" | custom-call | tf_op jit(solution)/shard_map/unpack/pallas_call | solution.py:95
  (51 shorter events, 9.2 us)
Async XLA Ops:
  0.6 94.7 %copy-start = (bf16[2,512,64]{1,2,0:T(8,128)(2,1)S(1)}, bf16[2,512,64]{1,2,0:T(8,128)(2,1)}, u32[]{:S(2)}) copy-start(bf16[2,512,64]{1,2,0:T(8,128)(2,1)} %param.13) | copy-start | bytes 393220
  1.8 2.2 %copy-start.2 = (bf16[1,2,128,8192]{3,2,1,0:T(8,128)(2,1)S(1)}, bf16[1,2,128,8192]{3,2,1,0:T(8,128)(2,1)}, u32[]{:S(2)}) copy-start(bf16[1,2,128,8192]{3,2,1,0:T(8,128)(2,1)} %param.8) | copy-start | bytes 12582916
  8.3 11.6 %copy-start.5 = (f32[1,64]{1,0:T(1,128)S(1)}, f32[1,64]{1,0:T(1,128)}, u32[]{:S(2)}) copy-start(f32[1,64]{1,0:T(1,128)} %param.12) | copy-start | bytes 772
  8.3 11.7 %copy-start.6 = (f32[1,64]{1,0:T(1,128)S(1)}, f32[1,64]{1,0:T(1,128)}, u32[]{:S(2)}) copy-start(f32[1,64]{1,0:T(1,128)} %param.11) | copy-start | bytes 772
  8.3 14.2 %copy-start.4 = (s32[2,8192]{1,0:T(2,128)S(1)}, s32[2,8192]{1,0:T(2,128)}, u32[]{:S(2)}) copy-start(s32[2,8192]{1,0:T(2,128)} %param.10) | copy-start | bytes 196612
  8.3 17.2 %copy-start.7 = (s32[2,512]{1,0:T(2,128)S(1)}, s32[2,512]{1,0:T(2,128)}, u32[]{:S(2)}) copy-start(s32[2,512]{1,0:T(2,128)} %param.9) | copy-start | bytes 12292
  8.3 32.8 %copy-start.3 = (bf16[2,512,64]{1,2,0:T(8,128)(2,1)S(1)}, bf16[2,512,64]{1,2,0:T(8,128)(2,1)}, u32[]{:S(2)}) copy-start(bf16[2,512,64]{1,2,0:T(8,128)(2,1)} %param.7) | copy-start | bytes 393220
  8.3 69.9 %all-to-all-start = ((bf16[128,144,128]{2,1,0:T(8,128)(2,1)}), bf16[128,144,128]{2,1,0:T(8,128)(2,1)}, u32[]{:S(2)}, u32[]{:S(2)}) async-start(bf16[128,144,128]{2,1,0:T(8,128)(2,1)} %pack.1), calls=%async_computation | async-start | bytes 9437184 | tf_op jit(solution)/shard_map/all_to_all | solution.py:549
  20.0 53.6 %collective-permute-start = (f32[2,64]{1,0:T(2,128)S(1)}, f32[2,64]{1,0:T(2,128)S(1)}, u32[]{:S(2)}, u32[]{:S(2)}) collective-permute-start(f32[2,64]{1,0:T(2,128)S(1)} %pad_maximum_fusion), channel_id=1, source_target_pairs={{0,64},{64,0},{1,65},{65,1},{2,66},{66,2},{3,67},{67,3},{4,68},{68... | collective-permute-start | bytes 1544 | tf_op jit(solution)/shard_map/ppermute | solution.py:532
  88.6 16.8 %all-to-all-start.1 = ((f32[64,1,1024]{2,1,0:T(1,128)}), f32[64,1,1024]{2,1,0:T(1,128)S(1)}, u32[]{:S(2)}, u32[]{:S(2)}) async-start(f32[64,1,1024]{2,1,0:T(1,128)} %copy.37), calls=%async_computation.1 | async-start | bytes 524288 | tf_op jit(solution)/shard_map/all_to_all | solution.py:536
  146.7 2.0 copy-start.1
  148.8 59.8 %all-to-all-start.3 = ((bf16[128,128,128]{2,1,0:T(8,128)(2,1)}), bf16[128,128,128]{2,1,0:T(8,128)(2,1)}, u32[]{:S(2)}, u32[]{:S(2)}) async-start(bf16[128,128,128]{2,1,0:T(8,128)(2,1)} %bitcast.69), calls=%async_computation.3 | async-start | bytes 8388608 | tf_op jit(solution)/shard_map/all_to_all | solution.py:575
  157.0 47.3 %collective-permute-start.1 = (bf16[512,64]{0,1:T(8,128)(2,1)S(1)}, bf16[512,64]{0,1:T(8,128)(2,1)S(1)}, u32[]{:S(2)}, u32[]{:S(2)}) collective-permute-start(bf16[512,64]{0,1:T(8,128)(2,1)S(1)} %get-tuple-element.51), channel_id=1, source_target_pairs={{0,64},{64,0},{1,65},{65,1},{2,66},{66,2},{3,67},{67,3},{4,68},{68... | collective-permute-start | bytes 196616 | tf_op jit(solution)/shard_map/ppermute | solution.py:532
  159.6 45.3 %collective-permute-start.2 = (f32[2,64]{1,0:T(2,128)S(1)}, f32[2,64]{1,0:T(2,128)S(1)}, u32[]{:S(2)}, u32[]{:S(2)}) collective-permute-start(f32[2,64]{1,0:T(2,128)S(1)} %select_bitcast_fusion.1), channel_id=1, source_target_pairs={{0,64},{64,0},{1,65},{65,1},{2,66},{66,2},{3,67},{67,3},{4,68},{68... | collective-permute-start | bytes 1544 | tf_op jit(solution)/shard_map/ppermute | solution.py:532
where the time goes:
time: 216 us
  waiting for transfers between devices  91.6 us (42%)
  Pallas kernels  47.6 us (22%)
  starting transfers between devices  31.4 us (15%)
  blocking collectives  14.1 us (7%)
  other arithmetic  13.4 us (6%)
  local copies, waits for them, and re-layouts  9.24 us (4%)
  between operations  5.83 us (3%)
  matrix products  2.28 us (1%)
    ppermute x3, waiting for transfers between devices, swap(): return lax.ppermute(value, 'phase', [(0, 1), (1, 0)])  74.9 us
    pallas_call x3, Pallas kernels, call(): pl.pallas_call(kernel, grid=(1,), in_specs=ins, out_specs=[spec for spec,...  36.3 us
    all_to_all x1, blocking collectives, spread(): return lax.all_to_all(value, 'seq', 0, 0, tiled=True)  14.1 us
    all_to_all x1, starting transfers between devices, local(): received = lax.all_to_all(sent, BOTH, 0, 0, tiled=True)  11.6 us
    all_to_all x1, waiting for transfers between devices, spread(): return lax.all_to_all(value, 'seq', 0, 0, tiled=True)  9.21 us
    pallas_call x1, Pallas kernels, unpack(): pl.pallas_call(unpack_kernel, grid=(micro * parts,), in_specs=[pl.BlockSp...  6.98 us
    all_to_all x1, starting transfers between devices, local(): lax.all_to_all(grad_kv.reshape(2 * blocks, 128, 128), BOTH, 0, 0, tiled=T...  6.89 us
    all_to_all x1, starting transfers between devices, spread(): return lax.all_to_all(value, 'seq', 0, 0, tiled=True)  6.76 us
  transfers between devices with their start and end apart: 6, of which 5 were waited for; matrix products, arithmetic and copies ran while one was open for 8% of the time, Pallas kernels for 0%

commit v1 on v0

v1 whole, which is shorter than its diff:
```python
import functools
import math

import jax
import jax.numpy as jnp
from jax import lax
from jax.experimental import pallas as pl
from jax.experimental.pallas import tpu as pltpu
from jax.sharding import PartitionSpec as P

D = 4096
HEAD = 64
EPS = 1e-06
NEG = -1e30
DOCS = 4
TILE = 256
CHUNK = 512
STEP1 = 10
STEP2 = 20
STEP3 = 5
GROUP = 8
VLIM = 60
TAIL = 16
SCALE = 1.0 / math.sqrt(HEAD)
LOG2 = SCALE * math.log2(math.e)
BOTH = ("phase", "seq")
F32 = jnp.float32
BF16 = jnp.bfloat16


def dot(a, b, ca, cb):
    return lax.dot_general(a, b, (((ca,), (cb,)), ((), ())), preferred_element_type=F32)


VMEM = pl.BlockSpec(memory_space=pltpu.VMEM)
SMEM = pl.BlockSpec(memory_space=pltpu.SMEM)
HBM = pl.BlockSpec(memory_space=pltpu.HBM)
PARAMS = dict(
    compiler_params=pltpu.CompilerParams(
        vmem_limit_bytes=VLIM * 1024 * 1024
    )
)


PIECES = 8


def pack_kernel(phase_ref, x_ref, kv_ref, out_ref, held, ready, in_sems, out_sems):
    per = out_ref.shape[0] // PIECES
    heads = kv_ref.shape[2] // 128
    arriving, leaving = [], []
    for i in range(PIECES):
        m, h = divmod(i * per, heads)
        source = kv_ref.at[m, :, pl.ds(h * 128, per * 128)]
        arriving.append(pltpu.make_async_copy(source, held.at[i], in_sems.at[i]))
        arriving[-1].start()
    tails = []
    for m in range(x_ref.shape[0]):
        half = pl.ds(pl.multiple_of(phase_ref[0] * 256, 256), 256)
        x = x_ref[m, :, half].astype(F32)
        rows = []
        for part in thirds(jnp.sum(x * x, axis=0, keepdims=True)):
            rows += [part[:, 0:128], part[:, 128:256]]
        rows.append(jnp.zeros((TAIL - 6, 128), F32))
        tails.append(jnp.concatenate(rows, axis=0).astype(BF16))
    for i in range(PIECES):
        arriving[i].wait()
        for j in range(per):
            ready[i * per + j, 0:128, :] = held[i, :, j * 128 : (j + 1) * 128]
            ready[i * per + j, 128 : 128 + TAIL, :] = tails[i * per // heads]
        piece = pl.ds(i * per, per)
        leaving.append(pltpu.make_async_copy(ready.at[piece], out_ref.at[piece], out_sems.at[i]))
        leaving[-1].start()
    for copy in leaving:
        copy.wait()


def pack(phase, kv, xts):
    micro, rows, feats = kv.shape
    count = micro * feats // 128
    shape = (count, rows + TAIL, 128)
    return pl.pallas_call(
        pack_kernel,
        in_specs=[SMEM, VMEM, HBM],
        out_specs=HBM,
        out_shape=jax.ShapeDtypeStruct(shape, BF16),
        scratch_shapes=[
            pltpu.VMEM((PIECES, rows, count // PIECES * 128), BF16),
            pltpu.VMEM(shape, BF16),
            pltpu.SemaphoreType.DMA((PIECES,)),
            pltpu.SemaphoreType.DMA((PIECES,)),
        ],
        name="pack",
        **PARAMS,
    )(phase, xts, kv)


def unpack_kernel(in_ref, out_ref, held, ready, in_sems, out_sems):
    per = in_ref.shape[0] // PIECES
    heads = out_ref.shape[2] // 128
    arriving, leaving = [], []
    for i in range(PIECES):
        piece = pl.ds(i * per, per)
        arriving.append(pltpu.make_async_copy(in_ref.at[piece], held.at[piece], in_sems.at[i]))
        arriving[-1].start()
    for i in range(PIECES):
        m, h = divmod(i * per, heads)
        arriving[i].wait()
        for j in range(per):
            ready[i, :, j * 128 : (j + 1) * 128] = held[i * per + j]
        target = out_ref.at[m, :, pl.ds(h * 128, per * 128)]
        leaving.append(pltpu.make_async_copy(ready.at[i], target, out_sems.at[i]))
        leaving[-1].start()
    for copy in leaving:
        copy.wait()


def unpack(blocks, micro):
    count, rows, _ = blocks.shape
    return pl.pallas_call(
        unpack_kernel,
        in_specs=[HBM],
        out_specs=HBM,
        out_shape=jax.ShapeDtypeStruct((micro, rows, count // micro * 128), BF16),
        scratch_shapes=[
            pltpu.VMEM(blocks.shape, BF16),
            pltpu.VMEM((PIECES, rows, count // PIECES * 128), BF16),
            pltpu.SemaphoreType.DMA((PIECES,)),
            pltpu.SemaphoreType.DMA((PIECES,)),
        ],
        name="unpack",
        **PARAMS,
    )(blocks)


def items_of(positions):
    return positions // CHUNK + DOCS


def fetches(received_ref, section, held, sems):
    copies = []
    for g in range(held.shape[0] // GROUP):
        piece = pl.ds(g * GROUP, GROUP)
        copies.append(
            pltpu.make_async_copy(
                received_ref.at[section, piece, pl.ds(0, 128), :], held.at[piece], sems.at[g]
            )
        )
        copies[-1].start()
    return copies


def work(kv_ref, body, step, before=None, after=None):
    items = items_of(kv_ref.shape[0] * 128)
    for start in range(0, items, step):
        stop = min(start + step, items)
        if before is not None:
            before(stop)
        for k in range(start, stop):
            body(k)
        if after is not None:
            after(stop, stop == items)


def halves(kv_ref, body, after):
    items = items_of(kv_ref.shape[0] * 128)
    step = items // 4

    def some(i, carry):
        for u in range(step):
            body(i * step + u)
        return carry

    lax.fori_loop(0, 2, some, 0)
    after(2 * step, False)
    lax.fori_loop(2, 4, some, 0)
    after(items, True)


def chunk_of(kv_ref, c):
    per = CHUNK // 128
    return kv_ref[pl.ds(c * per, per)].reshape(CHUNK, 128)


def lanes(d):
    return slice(d * TILE, (d + 1) * TILE)


def logits(product, c, first, last):
    position = lax.broadcasted_iota(jnp.int32, (CHUNK, TILE), 0) + c * CHUNK
    allowed = (position >= first) & (position < last)
    return jnp.where(allowed, product * LOG2, NEG)


def forward_items(plan_ref, kv_ref, copies, query, lse, total, query_ref, top_ref, norm_ref, store):
    for d in range(DOCS):
        query_ref[d] = query[:, lanes(d)]
    query_ref[DOCS] = jnp.zeros((128, TILE), BF16)
    top_ref[...] = jnp.full(top_ref.shape, NEG, F32)
    norm_ref[...] = jnp.zeros(norm_ref.shape, F32)
    total[...] = jnp.zeros(total.shape, F32)
    pending = list(copies)

    def stats(k):
        c, d = plan_ref[0, k], plan_ref[1, k]
        product = dot(chunk_of(kv_ref, c), query_ref[d], 1, 0)
        scores = logits(product, c, plan_ref[2, k], plan_ref[3, k])
        store[k] = scores
        groups = scores.reshape(CHUNK // 8, 8, TILE)
        top = jnp.max(groups, axis=0)
        norm = jnp.sum(jnp.exp2(groups - top[None]), axis=0)
        before = top_ref[d]
        now = jnp.maximum(before, top)
        norm_ref[d] = norm_ref[d] * jnp.exp2(before - now) + norm * jnp.exp2(top - now)
        top_ref[d] = now

    def arrived(stop):
        while pending and (len(copies) - len(pending)) * GROUP * 128 < stop * CHUNK:
            pending.pop(0).wait()

    work(kv_ref, stats, STEP1, before=arrived)
    for d in range(DOCS + 1):
        top = top_ref[d]
        peak = jnp.max(top, axis=0, keepdims=True)
        norm = jnp.sum(norm_ref[d] * jnp.exp2(top - peak), axis=0, keepdims=True)
        lse[d] = jnp.broadcast_to(peak + jnp.log2(norm), (8, TILE))

    def gather(k):
        c, d = plan_ref[0, k], plan_ref[1, k]
        probs = jnp.exp2(store[k] - lse[d, 0:1])
        weights = probs.astype(BF16)
        left = (probs - weights.astype(F32)).astype(BF16)
        total[d] += dot(chunk_of(kv_ref, c), jnp.concatenate([weights, left], axis=1), 0, 0)

    work(kv_ref, gather, STEP2)


def kv_scratch(blocks):
    return [
        pltpu.VMEM((blocks, 128, 128), BF16),
        pltpu.SemaphoreType.DMA((blocks // GROUP,)),
    ]


def forward_scratch(blocks):
    return [
        pltpu.VMEM((DOCS + 1, 128, 2 * TILE), F32),
        pltpu.VMEM((DOCS + 1, 128, TILE), BF16),
        pltpu.VMEM((DOCS + 1, 8, TILE), F32),
        pltpu.VMEM((DOCS + 1, 8, TILE), F32),
        pltpu.VMEM((items_of(blocks * 128), CHUNK, TILE), F32),
    ]


def attended(total, d):
    attn = total[d, HEAD:, :TILE]
    return attn, attn + total[d, HEAD:, TILE:]


def pad_low(a):
    return jnp.concatenate([a, jnp.zeros_like(a)], axis=0)


def pad_high(a):
    return jnp.concatenate([jnp.zeros_like(a), a], axis=0)


def upright(a):
    return jnp.transpose(a.astype(F32)).astype(BF16)


def normed_query(xt, total, qgain):
    inv = lax.rsqrt(total / D + EPS)
    return inv, (xt * inv * qgain).astype(BF16)


def as_messages(row, shape):
    tile = jnp.concatenate([row[:, 128 * j : 128 * j + 128] for j in range(shape[1])], axis=0)
    return jnp.broadcast_to(tile[None], shape)


def total_of(ref):
    tile = jnp.sum(ref[...], axis=0)
    return jnp.concatenate([tile[j : j + 1] for j in range(tile.shape[0])], axis=1)


def thirds(value):
    parts = []
    for _ in range(3):
        part = value.astype(BF16).astype(F32)
        parts.append(part)
        value = value - part
    return parts


def forward_kernel(
    plan_ref, xt_ref, row_ref, qgain_ref, ogain_ref, received_ref,
    out_ref, sums_ref, lse_ref, attn_ref, exact_ref, inv_ref,
    total_ref, query_ref, top_ref, norm_ref, store, kv_ref, sems, tails_ref, tails_sem,
):
    tails_copy = pltpu.make_async_copy(
        received_ref.at[:, :, pl.ds(128, TAIL), :], tails_ref, tails_sem
    )
    tails_copy.start()
    copies = fetches(received_ref, 0, kv_ref, sems)
    tails_copy.wait()
    tails = jnp.sum(tails_ref[...].astype(F32), axis=1)
    pieces = []
    for half in range(2):
        pieces += [
            tails[half, j : j + 1] + tails[half, j + 2 : j + 3] + tails[half, j + 4 : j + 5]
            for j in range(2)
        ]
    parts = thirds(jnp.concatenate(pieces, axis=1))
    parts.append(jnp.zeros((13, parts[0].shape[1]), F32))
    row = row_ref[...]
    rows = lax.broadcasted_iota(jnp.int32, (parts[0].shape[1], row.shape[1]), 0)
    place = jnp.where(rows == row, 1.0, 0.0).astype(BF16)
    moved = dot(jnp.concatenate(parts, axis=0).astype(BF16), place, 1, 0)
    total = jnp.sum(moved, axis=0, keepdims=True)
    xt = xt_ref[...].astype(F32)
    inv, query = normed_query(xt, total, qgain_ref[...])
    inv_ref[...] = inv
    forward_items(
        plan_ref, kv_ref, copies, pad_low(query), lse_ref, total_ref, query_ref, top_ref, norm_ref, store
    )
    for d in range(DOCS):
        s = lanes(d)
        attn, exact = attended(total_ref, d)
        attn_ref[:, s] = attn
        exact_ref[:, s] = exact
        out = xt[:, s] + ogain_ref[...] * attn
        out_ref[:, s] = jnp.where(row[:, s] >= 0, out, 0.0).astype(BF16)
    out = out_ref[...].astype(F32)
    sums_ref[...] = as_messages(jnp.sum(out * out, axis=0, keepdims=True), sums_ref.shape)


def call(kernel, name, ins, outs, scratch, args, **more):
    return pl.pallas_call(
        kernel,
        in_specs=ins,
        out_specs=[spec for spec, _ in outs],
        out_shape=[shape for _, shape in outs],
        scratch_shapes=scratch,
        name=name,
        **more,
        **PARAMS,
    )(*args)


def plain(shape, dtype=F32):
    return VMEM, jax.ShapeDtypeStruct(shape, dtype)


def forward(plan, received, xt, row, qgain, ogain):
    width = xt.shape[1]
    blocks = received.shape[1]
    outs = [
        plain((HEAD, width), BF16),
        plain((blocks, width // 128, 128)),
        plain((DOCS + 1, 8, TILE)),
        plain((HEAD, width)),
        plain((HEAD, width)),
        plain((1, width)),
    ]
    scratch = forward_scratch(blocks) + kv_scratch(blocks)
    scratch += [pltpu.VMEM((2, blocks, TAIL, 128), BF16), pltpu.SemaphoreType.DMA]
    return call(
        forward_kernel, "forward", [SMEM] + [VMEM] * 4 + [HBM], outs, scratch,
        (plan, xt, row, qgain, ogain, received),
    )


def backward_step(keyval, probs, grad_probs, delta, pair, grad_kv_ref, c):
    grad_scores = (probs * (grad_probs - delta)).astype(BF16)
    left = jnp.concatenate([grad_scores, probs.astype(BF16)], axis=1)
    per = CHUNK // 128
    held = grad_kv_ref[pl.ds(c * per, per)].reshape(CHUNK, 128)
    added = held.astype(F32) + dot(left, pair, 1, 0)
    grad_kv_ref[pl.ds(c * per, per)] = added.astype(BF16).reshape(per, 128, 128)
    return dot(keyval, grad_scores, 0, 0)[:HEAD]


class Leaving:
    def __init__(self, held, out_ref, section, sems):
        self.copies = []
        self.parts = (held, out_ref, section, sems)

    def after(self, stop, last):
        held, out_ref, section, sems = self.parts
        blocks = held.shape[0]
        done = blocks if last else max(0, stop - (DOCS - 1)) * (CHUNK // 128)
        while (len(self.copies) + 1) * GROUP <= done:
            g = len(self.copies)
            piece = pl.ds(g * GROUP, GROUP)
            copy = pltpu.make_async_copy(held.at[piece], out_ref.at[section, piece], sems.at[g])
            copy.start()
            self.copies.append(copy)

    def wait(self):
        for copy in self.copies:
            copy.wait()


def fill_pairs(pair_ref, delta_ref, query, grad_out, deltas):
    keys_side = upright(query.astype(F32) * SCALE)
    values_side = upright(grad_out)
    for d in range(DOCS):
        s = lanes(d)
        pair_ref[d] = jnp.concatenate([keys_side[s], values_side[s]], axis=0)
        delta_ref[d] = jnp.broadcast_to(deltas[:, s], (8, TILE))
    pair_ref[DOCS] = jnp.zeros((2 * TILE, 128), BF16)
    delta_ref[DOCS] = jnp.zeros((8, TILE), F32)


def backward_scratch():
    return [
        pltpu.VMEM((DOCS + 1, 2 * TILE, 128), BF16),
        pltpu.VMEM((DOCS + 1, 8, TILE), F32),
        pltpu.VMEM((DOCS + 1, HEAD, TILE), F32),
    ]


def lined_up(ref):
    return jnp.concatenate([ref[d] for d in range(DOCS)], axis=1)


def middle_kernel(
    plan_ref, sums_ref, xt_ref, qgain_ref, ogain_ref, gt_ref, received_ref,
    result_ref, out_ref, cross_ref, grad_norm_ref, inv_ref, grad_qg_ref, grad_og_ref,
    total_ref, query_ref, top_ref, norm_ref, store,
    pair_ref, delta_ref, grad_query_ref, lse_ref, grad_ref,
    kv_ref, sems, grad_kv_ref, out_sems,
):
    copies = fetches(received_ref, 1, kv_ref, sems)
    grad_kv_ref[...] = jnp.zeros_like(grad_kv_ref)
    grad_query_ref[...] = jnp.zeros_like(grad_query_ref)
    total = total_of(sums_ref)
    xt = xt_ref[...].astype(F32)
    inv, low = normed_query(xt, total, qgain_ref[...])
    inv_ref[...] = inv
    query = pad_low(low)
    grad = gt_ref[...].astype(F32)
    grad_low = (grad * ogain_ref[...]).astype(BF16)
    grad_out = pad_high(grad_low)
    for d in range(DOCS):
        grad_ref[d] = grad_out[:, lanes(d)]
    grad_ref[DOCS] = jnp.zeros((128, TILE), BF16)
    forward_items(
        plan_ref, kv_ref, copies, query, lse_ref, total_ref, query_ref, top_ref, norm_ref, store
    )
    both = [attended(total_ref, d) for d in range(DOCS)]
    attn = jnp.concatenate([a for a, _ in both], axis=1)
    exact = jnp.concatenate([e for _, e in both], axis=1)
    deltas = jnp.sum(grad_low.astype(F32) * exact, axis=0, keepdims=True)
    fill_pairs(pair_ref, delta_ref, query, grad_out, deltas)

    def back(k):
        c, d = plan_ref[0, k], plan_ref[1, k]
        keyval = chunk_of(kv_ref, c)
        probs = jnp.exp2(store[k] - lse_ref[d, 0:1])
        grad_probs = dot(keyval, grad_ref[d], 1, 0)
        grad_query_ref[d] += backward_step(
            keyval, probs, grad_probs, delta_ref[d, 0:1], pair_ref[d], grad_kv_ref, c
        )

    leaving = Leaving(grad_kv_ref, result_ref, 1, out_sems)
    halves(kv_ref, back, leaving.after)
    out_ref[...] = (xt + ogain_ref[...] * attn).astype(BF16)
    grad_query = lined_up(grad_query_ref) * SCALE
    grad_norm = grad_query * qgain_ref[...]
    grad_norm_ref[...] = grad_norm
    cross = jnp.sum(grad_norm * xt, axis=0, keepdims=True)
    cross_ref[...] = as_messages(cross, cross_ref.shape)
    grad_qg_ref[...] = jnp.sum(grad_query * (xt * inv), axis=1, keepdims=True)
    grad_og_ref[...] = jnp.sum(grad * attn, axis=1, keepdims=True)
    leaving.wait()


def middle(plan, received, sums, xt, qgain, ogain, gt):
    width = xt.shape[1]
    blocks = received.shape[1]
    outs = [
        (HBM, jax.ShapeDtypeStruct((2, blocks, 128, 128), BF16)),
        plain((HEAD, width), BF16),
        plain((blocks, width // 128, 128)),
        plain((HEAD, width)),
        plain((1, width)),
        plain((HEAD, 1)),
        plain((HEAD, 1)),
    ]
    scratch = forward_scratch(blocks) + backward_scratch()
    scratch += [
        pltpu.VMEM((DOCS + 1, 8, TILE), F32),
        pltpu.VMEM((DOCS + 1, 128, TILE), BF16),
    ]
    scratch += kv_scratch(blocks) + kv_scratch(blocks)
    return call(
        middle_kernel, "middle", [SMEM] + [VMEM] * 5 + [HBM], outs, scratch,
        (plan, sums, xt, qgain, ogain, gt, received),
    )


def backward_kernel(
    plan_ref, cross_ref, gt_ref, grad_norm_ref, xt1_ref, inv1_ref,
    xt_ref, inv_ref, lse_ref, attn_ref, exact_ref, qgain_ref, ogain_ref, received_ref, begun_ref,
    result_ref, grad_qg_ref, grad_og_ref, pair_ref, delta_ref, grad_query_ref, both_ref,
    kv_ref, sems, grad_kv_ref, out_sems,
):
    del begun_ref
    copies = fetches(received_ref, 0, kv_ref, sems)
    grad_kv_ref[...] = jnp.zeros_like(grad_kv_ref)
    grad_query_ref[...] = jnp.zeros_like(grad_query_ref)
    cross = total_of(cross_ref)
    inv1 = inv1_ref[...]
    xt1 = xt1_ref[...].astype(F32)
    grad = gt_ref[...].astype(F32) + inv1 * grad_norm_ref[...]
    grad = (grad - xt1 * (inv1 * inv1 * inv1) * (cross / D)).astype(BF16).astype(F32)
    grad_low = (grad * ogain_ref[...]).astype(BF16)
    grad_out = pad_high(grad_low)
    grad_og_ref[...] = jnp.sum(grad * attn_ref[...], axis=1, keepdims=True)
    deltas = jnp.sum(grad_low.astype(F32) * exact_ref[...], axis=0, keepdims=True)
    normed = xt_ref[...].astype(F32) * inv_ref[...]
    query = pad_low((normed * qgain_ref[...]).astype(BF16))
    fill_pairs(pair_ref, delta_ref, query, grad_out, deltas)
    for d in range(DOCS):
        both_ref[d] = jnp.concatenate([query[:, lanes(d)], grad_out[:, lanes(d)]], axis=1)
    both_ref[DOCS] = jnp.zeros((128, 2 * TILE), BF16)

    def back(k):
        c, d = plan_ref[0, k], plan_ref[1, k]
        keyval = chunk_of(kv_ref, c)
        product = dot(keyval, both_ref[d], 1, 0)
        scores = logits(product[:, :TILE], c, plan_ref[2, k], plan_ref[3, k])
        probs = jnp.exp2(scores - lse_ref[d, 0:1])
        grad_query_ref[d] += backward_step(
            keyval, probs, product[:, TILE:], delta_ref[d, 0:1], pair_ref[d], grad_kv_ref, c
        )

    for copy in copies:
        copy.wait()
    leaving = Leaving(grad_kv_ref, result_ref, 0, out_sems)
    halves(kv_ref, back, leaving.after)
    grad_query = lined_up(grad_query_ref) * SCALE
    grad_qg_ref[...] = jnp.sum(grad_query * normed, axis=1, keepdims=True)
    leaving.wait()


def backward(
    plan, received, cross, gt, grad_norm, xt1, inv1, xt, inv, lse, attn, exact, qgain, ogain, begun
):
    blocks = received.shape[1]
    outs = [
        (HBM, jax.ShapeDtypeStruct(begun.shape, BF16)),
        plain((HEAD, 1)),
        plain((HEAD, 1)),
    ]
    scratch = backward_scratch() + [pltpu.VMEM((DOCS + 1, 128, 2 * TILE), BF16)]
    scratch += kv_scratch(blocks) + kv_scratch(blocks)
    return call(
        backward_kernel, "backward", [SMEM] + [VMEM] * 12 + [HBM] * 2, outs, scratch,
        (plan, cross, gt, grad_norm, xt1, inv1, xt, inv, lse, attn, exact,
         qgain, ogain, received, begun),
        input_output_aliases={14: 0},
    )


def runs(seg):
    counts = [jnp.sum((seg < d).astype(jnp.int32)) for d in range(1, DOCS)]
    return jnp.stack([jnp.int32(0)] + counts + [jnp.int32(seg.shape[0])])


def plan_of(kseg):
    edges = runs(kseg)
    first, last = edges[:-1], edges[1:]
    start = first // CHUNK
    count = (last + (CHUNK - 1)) // CHUNK - start
    ends = jnp.cumsum(count)
    k = jnp.arange(items_of(kseg.shape[0]), dtype=jnp.int32)
    doc = jnp.sum((k[:, None] >= ends[None, :]).astype(jnp.int32), axis=1)
    chunk = jnp.full_like(k, kseg.shape[0] // CHUNK - 1)
    low, high = jnp.zeros_like(k), jnp.full_like(k, kseg.shape[0])
    for d in range(DOCS):
        here = doc == d
        chunk = jnp.where(here, start[d] + k - (ends[d] - count[d]), chunk)
        low = jnp.where(here, first[d], low)
        high = jnp.where(here, last[d], high)
    return jnp.stack([chunk, doc, low, high])


def place_of(qseg):
    edges = runs(qseg)
    lane = jnp.arange(TILE, dtype=jnp.int32)
    row = (edges[:-1, None] + lane[None, :]).reshape(1, DOCS * TILE)
    live = (lane[None, :] < (edges[1:] - edges[:-1])[:, None]).reshape(1, DOCS * TILE)
    rows = jnp.arange(qseg.shape[0], dtype=jnp.int32)[:, None]
    row = jnp.where(live, row, -1)
    return (rows == row).astype(BF16), row


def placed(x, place):
    return lax.dot_general(
        x, place, (((0,), (0,)), ((), ())), preferred_element_type=F32
    ).astype(BF16)


def taken(xt, place):
    return lax.dot_general(
        place, xt, (((1,), (1,)), ((), ())), preferred_element_type=F32
    ).astype(BF16)


def swap(value):
    return lax.ppermute(value, "phase", [(0, 1), (1, 0)])


def spread(value):
    return lax.all_to_all(value, "seq", 0, 0, tiled=True)


def local(dec_in, enc_kv, dec_seg, enc_seg, q_gain, o_gain, cotangent):
    phase = lax.axis_index("phase")
    first_phase = phase == 0
    micro = dec_in.shape[0]
    positions = enc_seg.shape[1]
    blocks = positions // 128

    sent = pack(phase.reshape(1), enc_kv[0], jnp.transpose(dec_in, (0, 2, 1)))
    own = jnp.concatenate([q_gain, o_gain], axis=0)
    other = swap(own)
    received = lax.all_to_all(sent, BOTH, 0, 0, tiled=True)
    received = received.reshape(2, blocks, 128 + TAIL, 128)

    gains0 = jnp.where(first_phase, own, other)
    gains1 = jnp.where(first_phase, other, own)
    qgain0, ogain0 = gains0[0][:, None], gains0[1][:, None]
    qgain1, ogain1 = gains1[0][:, None], gains1[1][:, None]
    qseg = lax.dynamic_index_in_dim(dec_seg, phase, 0, keepdims=False)
    kseg = lax.dynamic_index_in_dim(enc_seg, phase, 0, keepdims=False)
    plan = plan_of(kseg)
    place, row = place_of(qseg)
    xt0 = placed(lax.dynamic_index_in_dim(dec_in, phase, 0, keepdims=False), place)
    gt = placed(lax.dynamic_index_in_dim(cotangent, phase, 0, keepdims=False), place)

    xt1, sums, lse0, attn0, exact0, inv0 = forward(
        plan, received, xt0, row, qgain0, ogain0
    )
    sums = spread(sums)
    grad_kv, xt2, cross, grad_norm, inv1, grad_qg1, grad_og1 = middle(
        plan, received, sums, xt1, qgain1, ogain1, gt
    )
    cross = spread(cross)
    grad_kv, grad_qg0, grad_og0 = backward(
        plan, received, cross, gt, grad_norm, xt1, inv1, xt0, inv0, lse0, attn0, exact0,
        qgain0, ogain0, grad_kv,
    )
    rows_back = lax.all_to_all(
        grad_kv.reshape(2 * blocks, 128, 128), BOTH, 0, 0, tiled=True
    )
    grad_rows = unpack(rows_back, micro)

    out0, out1 = taken(xt1, place), taken(xt2, place)
    mine = jnp.where(first_phase, out0, out1)
    theirs = swap(jnp.where(first_phase, out1, out0))
    sect_out = jnp.where(
        first_phase, jnp.stack([mine, theirs]), jnp.stack([theirs, mine])
    )
    grads0 = jnp.concatenate([grad_qg0, grad_og0], axis=1).T
    grads1 = jnp.concatenate([grad_qg1, grad_og1], axis=1).T
    grads = jnp.where(first_phase, grads0, grads1) + swap(
        jnp.where(first_phase, grads1, grads0)
    )
    return (sect_out[None], grad_rows[None], grads[0:1], grads[1:2])


def solution(mesh):
    in_specs = (
        P(None, None, "seq"),
        P("phase", None, "seq", None),
        P(),
        P(),
        P("phase", "seq"),
        P("phase", "seq"),
        P(None, None, "seq"),
    )
    out_specs = (
        P("phase", None, None, "seq"),
        P("phase", None, "seq", None),
        P("phase", "seq"),
        P("phase", "seq"),
    )
    return jax.shard_map(local, mesh=mesh, in_specs=in_specs, out_specs=out_specs, check_vma=False)
```

time: 216 us -> 212 us (0.981)
  waiting for transfers between devices: 91.6 us -> 85.3 us
  local copies, waits for them, and re-layouts: 9.24 us -> 6.33 us
    unnamed x21 -> x28, local copies, waits for them, and re-layouts: 5.45 us -> 1.4 us
    ppermute x3, waiting for transfers between devices: 74.9 us -> 71.8 us  [swap(): return lax.ppermute(value, 'phase', [(0, 1), (1, 0)])]
  transfers between devices with their start and end apart: 6 -> 6, of which waited for: 5 -> 5; matrix products, arithmetic and copies ran while one was open for 8% -> 12% of each run, Pallas kernels for 0% -> 0%
where the time goes in v1:
time: 212 us; the launch traced here: 211 us
  waiting for transfers between devices  85.3 us (40%)
  Pallas kernels  47.9 us (23%)
  starting transfers between devices  31.6 us (15%)
  other arithmetic  15.5 us (7%)
  blocking collectives  15.3 us (7%)
  local copies, waits for them, and re-layouts  6.33 us (3%)
  between operations  6.05 us (3%)
  matrix products  3.32 us (2%)
    ppermute x3, waiting for transfers between devices, swap(): return lax.ppermute(value, 'phase', [(0, 1), (1, 0)])  71.8 us
    pallas_call x3, Pallas kernels, call(): pl.pallas_call(kernel, in_specs=ins, out_specs=[spec for spec, _ in outs]...  40 us
    all_to_all x1, blocking collectives, spread(): return lax.all_to_all(value, 'seq', 0, 0, tiled=True)  15.3 us
    all_to_all x1, starting transfers between devices, local(): received = lax.all_to_all(sent, BOTH, 0, 0, tiled=True)  11.6 us
    all_to_all x1, waiting for transfers between devices, spread(): return lax.all_to_all(value, 'seq', 0, 0, tiled=True)  7.25 us
    all_to_all x1, starting transfers between devices, spread(): return lax.all_to_all(value, 'seq', 0, 0, tiled=True)  6.95 us
    all_to_all x1, starting transfers between devices, local(): lax.all_to_all(grad_kv.reshape(2 * blocks, 128, 128), BOTH, 0, 0, tiled=T...  6.92 us
    ppermute x3, starting transfers between devices, swap(): return lax.ppermute(value, 'phase', [(0, 1), (1, 0)])  6.17 us
  transfers between devices with their start and end apart: 6, of which 5 were waited for; matrix products, arithmetic and copies ran while one was open for 12% of the time, Pallas kernels for 0%

profile of v1, /device:TPU:0, one launch (start us, length us, event | category | flops | bytes accessed | tf_op | source)
XLA Modules:
  0.0 211.4 jit_solution(12487453615890802377)
XLA Ops:
  0.7 4.5 %pack.1 = bf16[128,144,128]{2,1,0:T(8,128)(2,1)} custom-call(s32[1]{0:T(128)} %bitcast.26.phase_ref, bf16[2,64,512]{2,1,0:T(8,128)(2,1)} %bitcast.65, bf16[2,128,8192]{2,1,0:T(8,128)(2,1)} %bitcast.63), custom_call_target="tpu_custom_call" | custom-call | tf_op jit(solution)/shard_map/pack/pallas_call | solution.py:82
  5.2 11.6 %all-to-all-start = ((bf16[128,144,128]{2,1,0:T(8,128)(2,1)}), bf16[128,144,128]{2,1,0:T(8,128)(2,1)}, u32[]{:S(2)}, u32[]{:S(2)}) async-start(bf16[128,144,128]{2,1,0:T(8,128)(2,1)} %pack.1), calls=%async_computation | async-start | bytes 9437184 | tf_op jit(solution)/shard_map/all_to_all | solution.py:631
  16.9 2.5 %collective-permute-start = (f32[2,64]{1,0:T(2,128)S(1)}, f32[2,64]{1,0:T(2,128)S(1)}, u32[]{:S(2)}, u32[]{:S(2)}) collective-permute-start(f32[2,64]{1,0:T(2,128)S(1)} %pad_maximum_fusion), channel_id=1, source_target_pairs={{0,64},{64,0},{1,65},{65,1},{2,66},{66,2},{3,67},{67,3},{4,68},{68... | collective-permute-start | bytes 1544 | tf_op jit(solution)/shard_map/ppermute | solution.py:614
  20.1 2.0 fusion.36
  23.0 2.0 fusion.27
  25.0 2.0 add_subtract_fusion
  27.0 2.0 fusion.35
  35.4 4.4 %fusion.32 = (s32[1,20]{1,0:T(1,128)S(1)}, s32[1,20]{1,0:T(1,128)S(1)}, s32[1,20]{1,0:T(1,128)S(1)}) fusion(s32[]{:T(128)S(6)} %sub.106, s32[]{:T(128)} %bitcast.20, s32[]{:T(128)S(6)} %sub.103, s32[]{:T(128)} %bitcast.17, s32[]{:T(128)S(6)} %sub.100, s32[]{:T(128)} %bitcast.14, s32[]{:T(128)S(6)} %sub.97, s32[]{:T(128)} %bitcast.11, ...), kind=kLoop, calls=%fused_computation.75 | loop fusion | flops 460 | bytes 364 | tf_op jit(solution)/shard_map/jit(_where)/select_n | solution.py:585
  39.8 1.2 fusion.4.xt_ref
  42.2 28.3 %collective-permute-done = f32[2,64]{1,0:T(2,128)S(1)} collective-permute-done((f32[2,64]{1,0:T(2,128)S(1)}, f32[2,64]{1,0:T(2,128)S(1)}, u32[]{:S(2)}, u32[]{:S(2)}) %collective-permute-start) | collective-permute-done | bytes 544 | tf_op jit(solution)/shard_map/ppermute | solution.py:614
  71.9 3.2 %all-to-all-done = bf16[128,144,128]{2,1,0:T(8,128)(2,1)} async-done(((bf16[128,144,128]{2,1,0:T(8,128)(2,1)}), bf16[128,144,128]{2,1,0:T(8,128)(2,1)}, u32[]{:S(2)}, u32[]{:S(2)}) %all-to-all-start) | async-done | bytes 4718624 | tf_op jit(solution)/shard_map/all_to_all | solution.py:631
  75.1 10.2 %forward.1 = (bf16[64,1024]{1,0:T(8,128)(2,1)}, f32[64,8,128]{2,1,0:T(8,128)}, f32[5,8,256]{2,1,0:T(8,128)}, f32[64,1024]{1,0:T(8,128)}, f32[64,1024]{1,0:T(8,128)}, /*index=5*/f32[1,1024]{1,0:T(1,128)}) custom-call(s32[4,20]{1,0:T(4,128)} %pad_add_fusion.plan_ref, bf16[64,1024]{1,0:T(8,128)(2,1)} %fusion.4.xt_ref, s32[1,1024]{1,0:T(1,128)} %bitcast.67, ...), custom_call_target="tpu_custom_call" | custom-call | tf_op jit(solution)/shard_map/forward/pallas_call | solution.py:339
  85.3 7.0 %all-to-all-start.1 = ((f32[64,8,128]{2,1,0:T(8,128)}), f32[64,8,128]{2,1,0:T(8,128)S(1)}, u32[]{:S(2)}, u32[]{:S(2)}) async-start(f32[64,8,128]{2,1,0:T(8,128)} %get-tuple-element.21), calls=%async_computation.1 | async-start | bytes 524288 | tf_op jit(solution)/shard_map/all_to_all | solution.py:618
  92.2 1.2 fusion.5.gt_ref
  94.8 7.3 %all-to-all-done.1.sums_ref = f32[64,8,128]{2,1,0:T(8,128)S(1)} async-done(((f32[64,8,128]{2,1,0:T(8,128)}), f32[64,8,128]{2,1,0:T(8,128)S(1)}, u32[]{:S(2)}, u32[]{:S(2)}) %all-to-all-start.1) | async-done | bytes 262176 | tf_op jit(solution)/shard_map/all_to_all | solution.py:618
  102.8 17.7 %middle.1 = (bf16[2,64,128,128]{3,2,1,0:T(8,128)(2,1)}, bf16[64,1024]{1,0:T(8,128)(2,1)}, f32[64,8,128]{2,1,0:T(8,128)}, f32[64,1024]{1,0:T(8,128)}, f32[1,1024]...) custom-call(s32[4,20]{1,0:T(4,128)} %pad_add_fusion.plan_ref, f32[64,8,128]{2,1,0:T(8,128)} %copy-done.1, ...), custom_call_target="tpu_custom_call" | custom-call | tf_op jit(solution)/shard_map/middle/pallas_call | solution.py:339
  120.4 15.3 %all_to_all.20.cross_ref = f32[64,8,128]{2,1,0:T(8,128)} all-to-all(f32[64,8,128]{2,1,0:T(8,128)} %get-tuple-element.23), channel_id=1, replica_groups=mesh['phase'=2,'seq'=64] {'seq'}, dimensions={0} | all-to-all | bytes 524288 | tf_op jit(solution)/shard_map/all_to_all | solution.py:618
  135.8 12.2 %backward.1 = (bf16[2,64,128,128]{3,2,1,0:T(8,128)(2,1)}, f32[64,1]{1,0:T(8,128)}, f32[64,1]{1,0:T(8,128)}) custom-call(s32[4,20]{1,0:T(4,128)} %pad_add_fusion.plan_ref, f32[64,8,128]{2,1,0:T(8,128)} %all_to_all.20.cross_ref, bf16[64,1024]{1,0:T(8,128)(2,1)} %fusion.5.gt_ref, ...), custom_call_target="tpu_custom_call", output_to_operand_aliasing={{0}: (14, {})} | custom-call | tf_op jit(solution)/shard_map/backward/pallas_call | solution.py:339
  148.0 6.9 %all-to-all-start.3 = ((bf16[128,128,128]{2,1,0:T(8,128)(2,1)}), bf16[128,128,128]{2,1,0:T(8,128)(2,1)}, u32[]{:S(2)}, u32[]{:S(2)}) async-start(bf16[128,128,128]{2,1,0:T(8,128)(2,1)} %bitcast.62), calls=%async_computation.3 | async-start | bytes 8388608 | tf_op jit(solution)/shard_map/all_to_all | solution.py:657
  156.1 2.5 %collective-permute-start.1 = (bf16[512,64]{0,1:T(8,128)(2,1)S(1)}, bf16[512,64]{0,1:T(8,128)(2,1)S(1)}, u32[]{:S(2)}, u32[]{:S(2)}) collective-permute-start(bf16[512,64]{0,1:T(8,128)(2,1)S(1)} %get-tuple-element.49), channel_id=1, source_target_pairs={{0,64},{64,0},{1,65},{65,1},{2,66},{66,2},{3,67},{67,3},{4,68},{68... | collective-permute-start | bytes 196616 | tf_op jit(solution)/shard_map/ppermute | solution.py:614
  158.8 1.2 collective-permute-start.2
  160.0 43.6 %collective-permute-done.1 = bf16[512,64]{0,1:T(8,128)(2,1)S(1)} collective-permute-done((bf16[512,64]{0,1:T(8,128)(2,1)S(1)}, bf16[512,64]{0,1:T(8,128)(2,1)S(1)}, u32[]{:S(2)}, u32[]{:S(2)}) %collective-permute-start.1) | collective-permute-done | bytes 65568 | tf_op jit(solution)/shard_map/ppermute | solution.py:614
  204.8 3.1 %all-to-all-done.3.in_ref = bf16[128,128,128]{2,1,0:T(8,128)(2,1)} async-done(((bf16[128,128,128]{2,1,0:T(8,128)(2,1)}), bf16[128,128,128]{2,1,0:T(8,128)(2,1)}, u32[]{:S(2)}, u32[]{:S(2)}) %all-to-all-start.3) | async-done | bytes 4194336 | tf_op jit(solution)/shard_map/all_to_all | solution.py:657
  207.8 3.4 %unpack.1 = bf16[2,128,8192]{2,1,0:T(8,128)(2,1)} custom-call(bf16[128,128,128]{2,1,0:T(8,128)(2,1)} %all-to-all-done.3.in_ref), custom_call_target="tpu_custom_call" | custom-call | tf_op jit(solution)/shard_map/unpack/pallas_call | solution.py:120
  (54 shorter events, 10.5 us)
Async XLA Ops:
  0.6 91.6 %copy-start = (bf16[2,512,64]{1,2,0:T(8,128)(2,1)S(1)}, bf16[2,512,64]{1,2,0:T(8,128)(2,1)}, u32[]{:S(2)}) copy-start(bf16[2,512,64]{1,2,0:T(8,128)(2,1)} %param.13) | copy-start | bytes 393220
  5.1 11.7 %copy-start.9 = (f32[1,64]{1,0:T(1,128)S(1)}, f32[1,64]{1,0:T(1,128)}, u32[]{:S(2)}) copy-start(f32[1,64]{1,0:T(1,128)} %param.12) | copy-start | bytes 772
  5.1 11.7 %copy-start.10 = (f32[1,64]{1,0:T(1,128)S(1)}, f32[1,64]{1,0:T(1,128)}, u32[]{:S(2)}) copy-start(f32[1,64]{1,0:T(1,128)} %param.11) | copy-start | bytes 772
  5.2 14.2 %copy-start.8 = (s32[2,8192]{1,0:T(2,128)S(1)}, s32[2,8192]{1,0:T(2,128)}, u32[]{:S(2)}) copy-start(s32[2,8192]{1,0:T(2,128)} %param.10) | copy-start | bytes 196612
  5.2 17.2 %copy-start.11 = (s32[2,512]{1,0:T(2,128)S(1)}, s32[2,512]{1,0:T(2,128)}, u32[]{:S(2)}) copy-start(s32[2,512]{1,0:T(2,128)} %param.9) | copy-start | bytes 12292
  5.2 34.6 %copy-start.3 = (bf16[2,512,64]{1,2,0:T(8,128)(2,1)S(1)}, bf16[2,512,64]{1,2,0:T(8,128)(2,1)}, u32[]{:S(2)}) copy-start(bf16[2,512,64]{1,2,0:T(8,128)(2,1)} %param.7) | copy-start | bytes 393220
  5.2 69.9 %all-to-all-start = ((bf16[128,144,128]{2,1,0:T(8,128)(2,1)}), bf16[128,144,128]{2,1,0:T(8,128)(2,1)}, u32[]{:S(2)}, u32[]{:S(2)}) async-start(bf16[128,144,128]{2,1,0:T(8,128)(2,1)} %pack.1), calls=%async_computation | async-start | bytes 9437184 | tf_op jit(solution)/shard_map/all_to_all | solution.py:631
  16.9 53.6 %collective-permute-start = (f32[2,64]{1,0:T(2,128)S(1)}, f32[2,64]{1,0:T(2,128)S(1)}, u32[]{:S(2)}, u32[]{:S(2)}) collective-permute-start(f32[2,64]{1,0:T(2,128)S(1)} %pad_maximum_fusion), channel_id=1, source_target_pairs={{0,64},{64,0},{1,65},{65,1},{2,66},{66,2},{3,67},{67,3},{4,68},{68... | collective-permute-start | bytes 1544 | tf_op jit(solution)/shard_map/ppermute | solution.py:614
  85.3 16.8 %all-to-all-start.1 = ((f32[64,8,128]{2,1,0:T(8,128)}), f32[64,8,128]{2,1,0:T(8,128)S(1)}, u32[]{:S(2)}, u32[]{:S(2)}) async-start(f32[64,8,128]{2,1,0:T(8,128)} %get-tuple-element.21), calls=%async_computation.1 | async-start | bytes 524288 | tf_op jit(solution)/shard_map/all_to_all | solution.py:618
  102.0 0.7 copy-start.1
  148.0 7.0 %copy-start.2 = (bf16[64,1024]{1,0:T(8,128)(2,1)S(1)}, bf16[64,1024]{1,0:T(8,128)(2,1)}, u32[]{:S(2)}) copy-start(bf16[64,1024]{1,0:T(8,128)(2,1)} %get-tuple-element.20.xt_ref.xt1_ref) | copy-start | bytes 393220
  148.0 7.5 %copy-start.7 = (f32[64,1]{1,0:T(8,128)S(1)}, f32[64,1]{1,0:T(8,128)}, u32[]{:S(2)}) copy-start(f32[64,1]{1,0:T(8,128)} %get-tuple-element.34) | copy-start | bytes 772
  148.0 7.6 %copy-start.6 = (f32[64,1]{1,0:T(8,128)S(1)}, f32[64,1]{1,0:T(8,128)}, u32[]{:S(2)}) copy-start(f32[64,1]{1,0:T(8,128)} %get-tuple-element.35) | copy-start | bytes 772
  148.0 7.6 %copy-start.12 = (bf16[64,1024]{1,0:T(8,128)(2,1)S(1)}, bf16[64,1024]{1,0:T(8,128)(2,1)}, u32[]{:S(2)}) copy-start(bf16[64,1024]{1,0:T(8,128)(2,1)} %get-tuple-element.22) | copy-start | bytes 393220
  148.0 10.6 %copy-start.5 = (f32[64,1]{1,0:T(8,128)S(1)}, f32[64,1]{1,0:T(8,128)}, u32[]{:S(2)}) copy-start(f32[64,1]{1,0:T(8,128)} %get-tuple-element.32) | copy-start | bytes 772
  148.0 10.7 %copy-start.4 = (f32[64,1]{1,0:T(8,128)S(1)}, f32[64,1]{1,0:T(8,128)}, u32[]{:S(2)}) copy-start(f32[64,1]{1,0:T(8,128)} %get-tuple-element.33) | copy-start | bytes 772
  148.0 59.8 %all-to-all-start.3 = ((bf16[128,128,128]{2,1,0:T(8,128)(2,1)}), bf16[128,128,128]{2,1,0:T(8,128)(2,1)}, u32[]{:S(2)}, u32[]{:S(2)}) async-start(bf16[128,128,128]{2,1,0:T(8,128)(2,1)} %bitcast.62), calls=%async_computation.3 | async-start | bytes 8388608 | tf_op jit(solution)/shard_map/all_to_all | solution.py:657
  156.1 47.4 %collective-permute-start.1 = (bf16[512,64]{0,1:T(8,128)(2,1)S(1)}, bf16[512,64]{0,1:T(8,128)(2,1)S(1)}, u32[]{:S(2)}, u32[]{:S(2)}) collective-permute-start(bf16[512,64]{0,1:T(8,128)(2,1)S(1)} %get-tuple-element.49), channel_id=1, source_target_pairs={{0,64},{64,0},{1,65},{65,1},{2,66},{66,2},{3,67},{67,3},{4,68},{68... | collective-permute-start | bytes 196616 | tf_op jit(solution)/shard_map/ppermute | solution.py:614
  158.8 45.5 %collective-permute-start.2 = (f32[2,64]{1,0:T(2,128)S(1)}, f32[2,64]{1,0:T(2,128)S(1)}, u32[]{:S(2)}, u32[]{:S(2)}) collective-permute-start(f32[2,64]{1,0:T(2,128)S(1)} %select_bitcast_fusion.1), channel_id=1, source_target_pairs={{0,64},{64,0},{1,65},{65,1},{2,66},{66,2},{3,67},{67,3},{4,68},{68... | collective-permute-start | bytes 1544 | tf_op jit(solution)/shard_map/ppermute | solution.py:614

commit v2 on v0

--- a/solution.py
+++ b/solution.py
@@ -15,7 +15,7 @@
 DOCS = 4
 TILE = 256
 CHUNK = 512
-UNROLL = 4
+UNROLL = 10
 TAIL = 16
 SCALE = 1.0 / math.sqrt(HEAD)
 LOG2 = SCALE * math.log2(math.e)
@@ -39,67 +39,102 @@
 SMEM = pl.BlockSpec(memory_space=pltpu.SMEM)
 PARAMS = dict(
     compiler_params=pltpu.CompilerParams(
-        dimension_semantics=("arbitrary",), vmem_limit_bytes=48 * 1024 * 1024
+        dimension_semantics=("arbitrary",), vmem_limit_bytes=60 * 1024 * 1024
     )
 )
-
-
-def pack_kernel(phase_ref, kv_ref, x_ref, out_ref):
-    heads = kv_ref.shape[2] // (2 * HEAD)
-    for h in range(heads):
-        out_ref[h, 0:128, :] = kv_ref[0, :, h * 128 : (h + 1) * 128]
-    x = x_ref[0, pl.ds(phase_ref[0] * 256, 256), :].astype(F32)
-    x = jnp.concatenate([x, jnp.zeros_like(x)], axis=1)
-    xt = jnp.transpose(x)
-    total = jnp.sum(xt * xt, axis=0, keepdims=True)
-    rows = []
-    for _ in range(3):
-        part = total.astype(BF16)
-        partf = part.astype(F32)
-        rows += [partf[:, 0:128], partf[:, 128:256]]
-        total = total - partf
-    rows.append(jnp.zeros((TAIL - 6, 128), F32))
-    tail = jnp.concatenate(rows, axis=0).astype(BF16)
-    for h in range(heads):
-        out_ref[h, 128 : 128 + TAIL, :] = tail
-
-
-def pack(phase, kv, dec_in):
+SIMPLE = dict(compiler_params=pltpu.CompilerParams(vmem_limit_bytes=60 * 1024 * 1024))
+HBM = pl.BlockSpec(memory_space=pltpu.HBM)
+VMEM = pl.BlockSpec(memory_space=pltpu.VMEM)
+
+
+PIECES = 8
+
+
+def pack_kernel(phase_ref, x_ref, kv_ref, out_ref, held, ready, in_sems, out_sems):
+    per = out_ref.shape[0] // PIECES
+    heads = kv_ref.shape[2] // 128
+    arriving, leaving = [], []
+    for i in range(PIECES):
+        m, h = divmod(i * per, heads)
+        source = kv_ref.at[m, :, pl.ds(h * 128, per * 128)]
+        arriving.append(pltpu.make_async_copy(source, held.at[i], in_sems.at[i]))
+        arriving[-1].start()
+    tails = []
+    for m in range(x_ref.shape[0]):
+        half = pl.ds(pl.multiple_of(phase_ref[0] * 256, 256), 256)
+        x = x_ref[m, :, half].astype(F32)
+        rows = []
+        for part in thirds(jnp.sum(x * x, axis=0, keepdims=True)):
+            rows += [part[:, 0:128], part[:, 128:256]]
+        rows.append(jnp.zeros((TAIL - 6, 128), F32))
+        tails.append(jnp.concatenate(rows, axis=0).astype(BF16))
+    for i in range(PIECES):
+        arriving[i].wait()
+        for j in range(per):
+            ready[i * per + j, 0:128, :] = held[i, :, j * 128 : (j + 1) * 128]
+            ready[i * per + j, 128 : 128 + TAIL, :] = tails[i * per // heads]
+        piece = pl.ds(i * per, per)
+        leaving.append(pltpu.make_async_copy(ready.at[piece], out_ref.at[piece], out_sems.at[i]))
+        leaving[-1].start()
+    for copy in leaving:
+        copy.wait()
+
+
+def pack(phase, kv, xts):
     micro, rows, feats = kv.shape
-    parts = 4
-    heads = feats // 128 // parts
+    count = micro * feats // 128
+    shape = (count, rows + TAIL, 128)
     return pl.pallas_call(
         pack_kernel,
-        grid=(micro * parts,),
-        in_specs=[
-            SMEM,
-            pl.BlockSpec((1, rows, feats // parts), lambda i: (i // parts, 0, i % parts)),
-            pl.BlockSpec((1, dec_in.shape[1], HEAD), lambda i: (i // parts, 0, 0)),
+        in_specs=[SMEM, VMEM, HBM],
+        out_specs=HBM,
+        out_shape=jax.ShapeDtypeStruct(shape, BF16),
+        scratch_shapes=[
+            pltpu.VMEM((PIECES, rows, count // PIECES * 128), BF16),
+            pltpu.VMEM(shape, BF16),
+            pltpu.SemaphoreType.DMA((PIECES,)),
+            pltpu.SemaphoreType.DMA((PIECES,)),
         ],
-        out_specs=pl.BlockSpec((heads, rows + TAIL, 128), lambda i: (i, 0, 0)),
-        out_shape=jax.ShapeDtypeStruct((micro * parts * heads, rows + TAIL, 128), BF16),
         name="pack",
-        **PARAMS,
-    )(phase, kv, dec_in)
-
-
-def unpack_kernel(in_ref, out_ref):
-    for h in range(in_ref.shape[0]):
-        out_ref[0, :, h * 128 : (h + 1) * 128] = in_ref[h]
+        **SIMPLE,
+    )(phase, xts, kv)
+
+
+def unpack_kernel(in_ref, out_ref, held, ready, in_sems, out_sems):
+    per = in_ref.shape[0] // PIECES
+    heads = out_ref.shape[2] // 128
+    arriving, leaving = [], []
+    for i in range(PIECES):
+        piece = pl.ds(i * per, per)
+        arriving.append(pltpu.make_async_copy(in_ref.at[piece], held.at[piece], in_sems.at[i]))
+        arriving[-1].start()
+    for i in range(PIECES):
+        m, h = divmod(i * per, heads)
+        arriving[i].wait()
+        for j in range(per):
+            ready[i, :, j * 128 : (j + 1) * 128] = held[i * per + j]
+        target = out_ref.at[m, :, pl.ds(h * 128, per * 128)]
+        leaving.append(pltpu.make_async_copy(ready.at[i], target, out_sems.at[i]))
+        leaving[-1].start()
+    for copy in leaving:
+        copy.wait()
 
 
 def unpack(blocks, micro):
     count, rows, _ = blocks.shape
-    parts = 4
-    heads = count // micro // parts
     return pl.pallas_call(
         unpack_kernel,
-        grid=(micro * parts,),
-        in_specs=[pl.BlockSpec((heads, rows, 128), lambda i: (i, 0, 0))],
-        out_specs=pl.BlockSpec((1, rows, heads * 128), lambda i: (i // parts, 0, i % parts)),
-        out_shape=jax.ShapeDtypeStruct((micro, rows, parts * heads * 128), BF16),
+        in_specs=[HBM],
+        out_specs=HBM,
+        out_shape=jax.ShapeDtypeStruct((micro, rows, count // micro * 128), BF16),
+        scratch_shapes=[
+            pltpu.VMEM(blocks.shape, BF16),
+            pltpu.VMEM((PIECES, rows, count // PIECES * 128), BF16),
+            pltpu.SemaphoreType.DMA((PIECES,)),
+            pltpu.SemaphoreType.DMA((PIECES,)),
+        ],
         name="unpack",
-        **PARAMS,
+        **SIMPLE,
     )(blocks)
 
 
@@ -201,6 +236,16 @@
 def normed_query(xt, total, qgain):
     inv = lax.rsqrt(total / D + EPS)
     return inv, (xt * inv * qgain).astype(BF16)
+
+
+def as_messages(row, shape):
+    tile = jnp.concatenate([row[:, 128 * j : 128 * j + 128] for j in range(shape[1])], axis=0)
+    return jnp.broadcast_to(tile[None], shape)
+
+
+def total_of(ref):
+    tile = jnp.sum(ref[...], axis=0)
+    return jnp.concatenate([tile[j : j + 1] for j in range(tile.shape[0])], axis=1)
 
 
 def thirds(value):
@@ -242,7 +287,7 @@
         out = (xt[:, s] + ogain_ref[...] * attn) * live_ref[:, s]
         out_ref[:, s] = out.astype(BF16)
     out = out_ref[...].astype(F32)
-    sums_ref[...] = jnp.broadcast_to(jnp.sum(out * out, axis=0, keepdims=True), sums_ref.shape)
+    sums_ref[...] = as_messages(jnp.sum(out * out, axis=0, keepdims=True), sums_ref.shape)
 
 
 def call(kernel, name, ins, outs, scratch, args, **more):
@@ -278,7 +323,7 @@
     ]
     outs = [
         plain((HEAD, width), BF16),
-        plain((blocks, width)),
+        plain((blocks, width // 128, 128)),
         plain((DOCS + 1, 8, TILE)),
         plain((HEAD, width)),
         plain((HEAD, width)),
@@ -331,7 +376,7 @@
 ):
     grad_kv_ref[...] = jnp.zeros_like(grad_kv_ref)
     grad_query_ref[...] = jnp.zeros_like(grad_query_ref)
-    total = jnp.sum(sums_ref[...], axis=0, keepdims=True)
+    total = total_of(sums_ref)
     xt = xt_ref[...].astype(F32)
     inv, low = normed_query(xt, total, qgain_ref[...])
     inv_ref[...] = inv
@@ -366,7 +411,7 @@
     grad_norm = grad_query * qgain_ref[...]
     grad_norm_ref[...] = grad_norm
     cross = jnp.sum(grad_norm * xt, axis=0, keepdims=True)
-    cross_ref[...] = jnp.broadcast_to(cross, cross_ref.shape)
+    cross_ref[...] = as_messages(cross, cross_ref.shape)
     grad_qg_ref[...] = jnp.sum(grad_query * (xt * inv), axis=1, keepdims=True)
     grad_og_ref[...] = jnp.sum(grad * attn, axis=1, keepdims=True)
 
@@ -377,7 +422,7 @@
     ins = [
         SMEM,
         vmem((1, blocks, 128, 128), (1, 0, 0, 0)),
-        whole((blocks, width)),
+        whole((blocks, width // 128, 128)),
         whole((HEAD, width)),
         whole((1, width)),
         whole((HEAD, 1)),
@@ -390,7 +435,7 @@
             jax.ShapeDtypeStruct((2, blocks, 128, 128), BF16),
         ),
         plain((HEAD, width), BF16),
-        plain((blocks, width)),
+        plain((blocks, width // 128, 128)),
         plain((HEAD, width)),
         plain((1, width)),
         plain((HEAD, 1)),
@@ -415,7 +460,7 @@
     del held_ref
     grad_kv_ref[...] = jnp.zeros_like(grad_kv_ref)
     grad_query_ref[...] = jnp.zeros_like(grad_query_ref)
-    cross = jnp.sum(cross_ref[...], axis=0, keepdims=True)
+    cross = total_of(cross_ref)
     inv1 = inv1_ref[...]
     xt1 = xt1_ref[...].astype(F32)
     grad = gt_ref[...].astype(F32) + inv1 * grad_norm_ref[...]
@@ -454,7 +499,7 @@
     ins = [
         SMEM,
         vmem((1, blocks, 128, 128), (0, 0, 0, 0)),
-        whole((blocks, width)),
+        whole((blocks, width // 128, 128)),
         whole((HEAD, width)),
         whole((HEAD, width)),
         whole((HEAD, width)),
@@ -543,7 +588,7 @@
     positions = enc_seg.shape[1]
     blocks = positions // 128
 
-    sent = pack(phase.reshape(1), enc_kv[0], dec_in)
+    sent = pack(phase.reshape(1), enc_kv[0], jnp.transpose(dec_in, (0, 2, 1)))
     own = jnp.concatenate([q_gain, o_gain], axis=0)
     other = swap(own)
     received = lax.all_to_all(sent, BOTH, 0, 0, tiled=True)

time: 216 us -> 210 us (0.972)
  waiting for transfers between devices: 91.6 us -> 85.4 us
  local copies, waits for them, and re-layouts: 9.24 us -> 6.34 us
  Pallas kernels: 47.6 us -> 45.4 us
    unnamed x21 -> x28, local copies, waits for them, and re-layouts: 5.45 us -> 1.38 us
    pallas_call x2, Pallas kernels: 11.3 us -> 7.86 us  [the longest x1 4.48 us: pack(): pl.pallas_call(pack_kernel, in_specs=[SMEM, VMEM, HBM], out_specs=HBM, ou...]
    ppermute x3, waiting for transfers between devices: 74.9 us -> 72 us  [swap(): return lax.ppermute(value, 'phase', [(0, 1), (1, 0)])]
  transfers between devices with their start and end apart: 6 -> 6, of which waited for: 5 -> 5; matrix products, arithmetic and copies ran while one was open for 8% -> 12% of each run, Pallas kernels for 0% -> 0%
where the time goes in v2:
time: 210 us; the launch traced here: 209 us
  waiting for transfers between devices  85.4 us (41%)
  Pallas kernels  45.4 us (22%)
  starting transfers between devices  31.6 us (15%)
  blocking collectives  15.4 us (7%)
  other arithmetic  15 us (7%)
  local copies, waits for them, and re-layouts  6.34 us (3%)
  between operations  6.07 us (3%)
  matrix products  3.61 us (2%)
    ppermute x3, waiting for transfers between devices, swap(): return lax.ppermute(value, 'phase', [(0, 1), (1, 0)])  72 us
    pallas_call x3, Pallas kernels, call(): pl.pallas_call(kernel, grid=(1,), in_specs=ins, out_specs=[spec for spec,...  37.5 us
    all_to_all x1, blocking collectives, spread(): return lax.all_to_all(value, 'seq', 0, 0, tiled=True)  15.4 us
    all_to_all x1, starting transfers between devices, local(): received = lax.all_to_all(sent, BOTH, 0, 0, tiled=True)  11.6 us
    all_to_all x1, waiting for transfers between devices, spread(): return lax.all_to_all(value, 'seq', 0, 0, tiled=True)  7.15 us
    all_to_all x1, starting transfers between devices, spread(): return lax.all_to_all(value, 'seq', 0, 0, tiled=True)  6.92 us
    all_to_all x1, starting transfers between devices, local(): lax.all_to_all(grad_kv.reshape(2 * blocks, 128, 128), BOTH, 0, 0, tiled=T...  6.92 us
    ppermute x3, starting transfers between devices, swap(): return lax.ppermute(value, 'phase', [(0, 1), (1, 0)])  6.17 us
  transfers between devices with their start and end apart: 6, of which 5 were waited for; matrix products, arithmetic and copies ran while one was open for 12% of the time, Pallas kernels for 0%

profile of v2, /device:TPU:0, one launch (start us, length us, event | category | flops | bytes accessed | tf_op | source)
XLA Modules:
  0.0 208.8 jit_solution(4301150521465594721)
XLA Ops:
  0.7 4.5 %pack.1 = bf16[128,144,128]{2,1,0:T(8,128)(2,1)} custom-call(s32[1]{0:T(128)} %bitcast.23.phase_ref, bf16[2,64,512]{2,1,0:T(8,128)(2,1)} %bitcast.65, bf16[2,128,8192]{2,1,0:T(8,128)(2,1)} %bitcast.63), custom_call_target="tpu_custom_call" | custom-call | tf_op jit(solution)/shard_map/pack/pallas_call | solution.py:87
  5.2 11.6 %all-to-all-start = ((bf16[128,144,128]{2,1,0:T(8,128)(2,1)}), bf16[128,144,128]{2,1,0:T(8,128)(2,1)}, u32[]{:S(2)}, u32[]{:S(2)}) async-start(bf16[128,144,128]{2,1,0:T(8,128)(2,1)} %pack.1), calls=%async_computation | async-start | bytes 9437184 | tf_op jit(solution)/shard_map/all_to_all | solution.py:594
  16.9 2.5 %collective-permute-start = (f32[2,64]{1,0:T(2,128)S(1)}, f32[2,64]{1,0:T(2,128)S(1)}, u32[]{:S(2)}, u32[]{:S(2)}) collective-permute-start(f32[2,64]{1,0:T(2,128)S(1)} %pad_maximum_fusion), channel_id=1, source_target_pairs={{0,64},{64,0},{1,65},{65,1},{2,66},{66,2},{3,67},{67,3},{4,68},{68... | collective-permute-start | bytes 1544 | tf_op jit(solution)/shard_map/ppermute | solution.py:577
  20.1 2.0 fusion.52
  23.1 2.0 add_subtract_fusion
  25.3 2.0 fusion.51
  33.7 4.4 %fusion.48 = (s32[1,20]{1,0:T(1,128)S(1)}, s32[1,20]{1,0:T(1,128)S(1)}, s32[1,20]{1,0:T(1,128)S(1)}) fusion(s32[]{:T(128)S(6)} %sub.106, s32[]{:T(128)} %bitcast.20, s32[]{:T(128)S(6)} %sub.103, s32[]{:T(128)} %bitcast.17, s32[]{:T(128)S(6)} %sub.100, s32[]{:T(128)} %bitcast.14, s32[]{:T(128)S(6)} %sub.97, s32[]{:T(128)} %bitcast.11, ...), kind=kLoop, calls=%fused_computation.80 | loop fusion | flops 460 | bytes 364 | tf_op jit(solution)/shard_map/jit(_where)/select_n | solution.py:549
  38.1 1.2 fusion.10.xt_ref
  39.3 1.4 fusion.7.place_ref
  41.9 28.6 %collective-permute-done = f32[2,64]{1,0:T(2,128)S(1)} collective-permute-done((f32[2,64]{1,0:T(2,128)S(1)}, f32[2,64]{1,0:T(2,128)S(1)}, u32[]{:S(2)}, u32[]{:S(2)}) %collective-permute-start) | collective-permute-done | bytes 544 | tf_op jit(solution)/shard_map/ppermute | solution.py:577
  71.9 3.2 %all-to-all-done = bf16[128,144,128]{2,1,0:T(8,128)(2,1)} async-done(((bf16[128,144,128]{2,1,0:T(8,128)(2,1)}), bf16[128,144,128]{2,1,0:T(8,128)(2,1)}, u32[]{:S(2)}, u32[]{:S(2)}) %all-to-all-start) | async-done | bytes 4718624 | tf_op jit(solution)/shard_map/all_to_all | solution.py:594
  75.1 9.7 %forward.1 = (bf16[64,1024]{1,0:T(8,128)(2,1)}, f32[64,8,128]{2,1,0:T(8,128)}, f32[5,8,256]{2,1,0:T(8,128)}, f32[64,1024]{1,0:T(8,128)}, f32[64,1024]{1,0:T(8,128)}, /*index=5*/f32[1,1024]{1,0:T(1,128)}) custom-call(s32[4,20]{1,0:T(4,128)} %pad_add_fusion.plan_ref, bf16[2,64,144,128]{3,2,1,0:T(8,128)(2,1)} %bitcast.26.kv_ref.tails_ref, ...), custom_call_target="tpu_custom_call" | custom-call | tf_op jit(solution)/shard_map/forward/pallas_call | solution.py:294
  84.7 6.9 %all-to-all-start.1 = ((f32[64,8,128]{2,1,0:T(8,128)}), f32[64,8,128]{2,1,0:T(8,128)S(1)}, u32[]{:S(2)}, u32[]{:S(2)}) async-start(f32[64,8,128]{2,1,0:T(8,128)} %get-tuple-element.21), calls=%async_computation.1 | async-start | bytes 524288 | tf_op jit(solution)/shard_map/all_to_all | solution.py:581
  91.7 1.2 fusion.13.gt_ref
  94.3 7.2 %all-to-all-done.1.sums_ref = f32[64,8,128]{2,1,0:T(8,128)S(1)} async-done(((f32[64,8,128]{2,1,0:T(8,128)}), f32[64,8,128]{2,1,0:T(8,128)S(1)}, u32[]{:S(2)}, u32[]{:S(2)}) %all-to-all-start.1) | async-done | bytes 262176 | tf_op jit(solution)/shard_map/all_to_all | solution.py:581
  102.2 16.9 %middle.1 = (bf16[2,64,128,128]{3,2,1,0:T(8,128)(2,1)}, bf16[64,1024]{1,0:T(8,128)(2,1)}, f32[64,8,128]{2,1,0:T(8,128)}, f32[64,1024]{1,0:T(8,128)}, f32[1,1024]...) custom-call(s32[4,20]{1,0:T(4,128)} %pad_add_fusion.plan_ref, bf16[2,64,144,128]{3,2,1,0:T(8,128)(2,1)} %bitcast.26.kv_ref.tails_ref, ...), custom_call_target="tpu_custom_call" | custom-call | tf_op jit(solution)/shard_map/middle/pallas_call | solution.py:294
  119.1 15.4 %all_to_all.20.cross_ref = f32[64,8,128]{2,1,0:T(8,128)} all-to-all(f32[64,8,128]{2,1,0:T(8,128)} %get-tuple-element.23), channel_id=1, replica_groups=mesh['phase'=2,'seq'=64] {'seq'}, dimensions={0} | all-to-all | bytes 524288 | tf_op jit(solution)/shard_map/all_to_all | solution.py:581
  134.5 10.9 %backward.1 = (bf16[2,64,128,128]{3,2,1,0:T(8,128)(2,1)}, f32[64,1]{1,0:T(8,128)}, f32[64,1]{1,0:T(8,128)}) custom-call(s32[4,20]{1,0:T(4,128)} %pad_add_fusion.plan_ref, bf16[2,64,144,128]{3,2,1,0:T(8,128)(2,1)} %bitcast.26.kv_ref.tails_ref, f32[64,8,128]{2,1,0:T(8,128)} %all_to_all.20.cross_ref, ...), custom_call_target="tpu_custom_call", output_to_operand_aliasing={{0}: (14, {})} | custom-call | tf_op jit(solution)/shard_map/backward/pallas_call | solution.py:294
  145.4 6.9 %all-to-all-start.3 = ((bf16[128,128,128]{2,1,0:T(8,128)(2,1)}), bf16[128,128,128]{2,1,0:T(8,128)(2,1)}, u32[]{:S(2)}, u32[]{:S(2)}) async-start(bf16[128,128,128]{2,1,0:T(8,128)(2,1)} %bitcast.62), calls=%async_computation.3 | async-start | bytes 8388608 | tf_op jit(solution)/shard_map/all_to_all | solution.py:620
  153.7 2.5 %collective-permute-start.1 = (bf16[512,64]{0,1:T(8,128)(2,1)S(1)}, bf16[512,64]{0,1:T(8,128)(2,1)S(1)}, u32[]{:S(2)}, u32[]{:S(2)}) collective-permute-start(bf16[512,64]{0,1:T(8,128)(2,1)S(1)} %get-tuple-element.51), channel_id=1, source_target_pairs={{0,64},{64,0},{1,65},{65,1},{2,66},{66,2},{3,67},{67,3},{4,68},{68... | collective-permute-start | bytes 196616 | tf_op jit(solution)/shard_map/ppermute | solution.py:577
  156.4 1.2 collective-permute-start.2
  157.6 43.4 %collective-permute-done.1 = bf16[512,64]{0,1:T(8,128)(2,1)S(1)} collective-permute-done((bf16[512,64]{0,1:T(8,128)(2,1)S(1)}, bf16[512,64]{0,1:T(8,128)(2,1)S(1)}, u32[]{:S(2)}, u32[]{:S(2)}) %collective-permute-start.1) | collective-permute-done | bytes 65568 | tf_op jit(solution)/shard_map/ppermute | solution.py:577
  202.2 3.1 %all-to-all-done.3.in_ref = bf16[128,128,128]{2,1,0:T(8,128)(2,1)} async-done(((bf16[128,128,128]{2,1,0:T(8,128)(2,1)}), bf16[128,128,128]{2,1,0:T(8,128)(2,1)}, u32[]{:S(2)}, u32[]{:S(2)}) %all-to-all-start.3) | async-done | bytes 4194336 | tf_op jit(solution)/shard_map/all_to_all | solution.py:620
  205.3 3.4 %unpack.1 = bf16[2,128,8192]{2,1,0:T(8,128)(2,1)} custom-call(bf16[128,128,128]{2,1,0:T(8,128)(2,1)} %all-to-all-done.3.in_ref), custom_call_target="tpu_custom_call" | custom-call | tf_op jit(solution)/shard_map/unpack/pallas_call | solution.py:125
  (56 shorter events, 10.7 us)
Async XLA Ops:
  0.6 91.0 %copy-start = (bf16[2,512,64]{1,2,0:T(8,128)(2,1)S(1)}, bf16[2,512,64]{1,2,0:T(8,128)(2,1)}, u32[]{:S(2)}) copy-start(bf16[2,512,64]{1,2,0:T(8,128)(2,1)} %param.13) | copy-start | bytes 393220
  5.1 11.7 %copy-start.9 = (f32[1,64]{1,0:T(1,128)S(1)}, f32[1,64]{1,0:T(1,128)}, u32[]{:S(2)}) copy-start(f32[1,64]{1,0:T(1,128)} %param.12) | copy-start | bytes 772
  5.2 11.7 %copy-start.10 = (f32[1,64]{1,0:T(1,128)S(1)}, f32[1,64]{1,0:T(1,128)}, u32[]{:S(2)}) copy-start(f32[1,64]{1,0:T(1,128)} %param.11) | copy-start | bytes 772
  5.2 14.2 %copy-start.8 = (s32[2,8192]{1,0:T(2,128)S(1)}, s32[2,8192]{1,0:T(2,128)}, u32[]{:S(2)}) copy-start(s32[2,8192]{1,0:T(2,128)} %param.10) | copy-start | bytes 196612
  5.2 17.2 %copy-start.11 = (s32[2,512]{1,0:T(2,128)S(1)}, s32[2,512]{1,0:T(2,128)}, u32[]{:S(2)}) copy-start(s32[2,512]{1,0:T(2,128)} %param.9) | copy-start | bytes 12292
  5.2 32.9 %copy-start.3 = (bf16[2,512,64]{1,2,0:T(8,128)(2,1)S(1)}, bf16[2,512,64]{1,2,0:T(8,128)(2,1)}, u32[]{:S(2)}) copy-start(bf16[2,512,64]{1,2,0:T(8,128)(2,1)} %param.7) | copy-start | bytes 393220
  5.2 69.9 %all-to-all-start = ((bf16[128,144,128]{2,1,0:T(8,128)(2,1)}), bf16[128,144,128]{2,1,0:T(8,128)(2,1)}, u32[]{:S(2)}, u32[]{:S(2)}) async-start(bf16[128,144,128]{2,1,0:T(8,128)(2,1)} %pack.1), calls=%async_computation | async-start | bytes 9437184 | tf_op jit(solution)/shard_map/all_to_all | solution.py:594
  16.9 53.6 %collective-permute-start = (f32[2,64]{1,0:T(2,128)S(1)}, f32[2,64]{1,0:T(2,128)S(1)}, u32[]{:S(2)}, u32[]{:S(2)}) collective-permute-start(f32[2,64]{1,0:T(2,128)S(1)} %pad_maximum_fusion), channel_id=1, source_target_pairs={{0,64},{64,0},{1,65},{65,1},{2,66},{66,2},{3,67},{67,3},{4,68},{68... | collective-permute-start | bytes 1544 | tf_op jit(solution)/shard_map/ppermute | solution.py:577
  84.7 16.7 %all-to-all-start.1 = ((f32[64,8,128]{2,1,0:T(8,128)}), f32[64,8,128]{2,1,0:T(8,128)S(1)}, u32[]{:S(2)}, u32[]{:S(2)}) async-start(f32[64,8,128]{2,1,0:T(8,128)} %get-tuple-element.21), calls=%async_computation.1 | async-start | bytes 524288 | tf_op jit(solution)/shard_map/all_to_all | solution.py:581
  101.5 0.7 copy-start.1
  145.4 7.0 %copy-start.2 = (bf16[64,1024]{1,0:T(8,128)(2,1)S(1)}, bf16[64,1024]{1,0:T(8,128)(2,1)}, u32[]{:S(2)}) copy-start(bf16[64,1024]{1,0:T(8,128)(2,1)} %get-tuple-element.20.xt_ref.xt1_ref) | copy-start | bytes 393220
  145.4 7.6 %copy-start.7 = (f32[64,1]{1,0:T(8,128)S(1)}, f32[64,1]{1,0:T(8,128)}, u32[]{:S(2)}) copy-start(f32[64,1]{1,0:T(8,128)} %get-tuple-element.34) | copy-start | bytes 772
  145.4 7.6 %copy-start.6 = (f32[64,1]{1,0:T(8,128)S(1)}, f32[64,1]{1,0:T(8,128)}, u32[]{:S(2)}) copy-start(f32[64,1]{1,0:T(8,128)} %get-tuple-element.35) | copy-start | bytes 772
  145.4 7.7 %copy-start.12 = (bf16[64,1024]{1,0:T(8,128)(2,1)S(1)}, bf16[64,1024]{1,0:T(8,128)(2,1)}, u32[]{:S(2)}) copy-start(bf16[64,1024]{1,0:T(8,128)(2,1)} %get-tuple-element.22) | copy-start | bytes 393220
  145.4 59.8 %all-to-all-start.3 = ((bf16[128,128,128]{2,1,0:T(8,128)(2,1)}), bf16[128,128,128]{2,1,0:T(8,128)(2,1)}, u32[]{:S(2)}, u32[]{:S(2)}) async-start(bf16[128,128,128]{2,1,0:T(8,128)(2,1)} %bitcast.62), calls=%async_computation.3 | async-start | bytes 8388608 | tf_op jit(solution)/shard_map/all_to_all | solution.py:620
  152.4 3.8 %copy-start.5 = (f32[64,1]{1,0:T(8,128)S(1)}, f32[64,1]{1,0:T(8,128)}, u32[]{:S(2)}) copy-start(f32[64,1]{1,0:T(8,128)} %get-tuple-element.32) | copy-start | bytes 772
  152.4 3.9 %copy-start.4 = (f32[64,1]{1,0:T(8,128)S(1)}, f32[64,1]{1,0:T(8,128)}, u32[]{:S(2)}) copy-start(f32[64,1]{1,0:T(8,128)} %get-tuple-element.33) | copy-start | bytes 772
  153.7 47.3 %collective-permute-start.1 = (bf16[512,64]{0,1:T(8,128)(2,1)S(1)}, bf16[512,64]{0,1:T(8,128)(2,1)S(1)}, u32[]{:S(2)}, u32[]{:S(2)}) collective-permute-start(bf16[512,64]{0,1:T(8,128)(2,1)S(1)} %get-tuple-element.51), channel_id=1, source_target_pairs={{0,64},{64,0},{1,65},{65,1},{2,66},{66,2},{3,67},{67,3},{4,68},{68... | collective-permute-start | bytes 196616 | tf_op jit(solution)/shard_map/ppermute | solution.py:577
  156.4 45.3 %collective-permute-start.2 = (f32[2,64]{1,0:T(2,128)S(1)}, f32[2,64]{1,0:T(2,128)S(1)}, u32[]{:S(2)}, u32[]{:S(2)}) collective-permute-start(f32[2,64]{1,0:T(2,128)S(1)} %select_bitcast_fusion.1), channel_id=1, source_target_pairs={{0,64},{64,0},{1,65},{65,1},{2,66},{66,2},{3,67},{67,3},{4,68},{68... | collective-permute-start | bytes 1544 | tf_op jit(solution)/shard_map/ppermute | solution.py:577
